TPU v7x, 256 devices: a whole 4x4x8 slice. The times are simulated.
256 devices in a mesh: band: 8 (over x, z_lo), dom: 32 (over z_hi, y, core).
Axes of the slice: x: 4, y: 4, z: 8 (z_hi: 4, z_lo: 2; z = z_hi * 2 + z_lo), core: 2. Of those that a mesh axis runs over, the one named last changes fastest.
Arguments:
- orbitals: float32 [128, 128, 32, 128], P('band', 'dom'), may hold values from -6 to 6
- potential: float32 [128, 32, 128], P('dom'), may hold values from 0 to 1.5
Outputs:
- rotated: float32 [128, 128, 32, 128], P('band', 'dom')
All inputs are finite; a program needn't handle non-finite values.
Results may differ from a plain program's by a relative error of at most 0.0043.
Values may be sent and summed in bfloat16 or wider, within the bound.
A program may use at most 128 MiB of HBM per device.

v0:
```python
import jax
import jax.numpy as jnp
from jax import lax
from jax.sharding import PartitionSpec as P

DEGREE = 6


centre = 5.5
half = 4.5


def extended_2(cells, sides, width):
    for axis, dim in sides:
        count = lax.axis_size(axis)
        head = lax.slice_in_dim(cells, 0, width, axis=dim)
        tail = lax.slice_in_dim(cells, cells.shape[dim] - width, cells.shape[dim], axis=dim)
        cells = jnp.concatenate(
            [
                lax.ppermute(tail, axis, [(i, (i + 1) % count) for i in range(count)]),
                cells,
                lax.ppermute(head, axis, [((i + 1) % count, i) for i in range(count)]),
            ],
            axis=dim,
        )
    return cells


def stencil(extended, potential):
    count = extended.shape[1] - 4
    middle = extended[:, 2 : 2 + count]
    lap = -7.5 * middle
    lap = lap + 4.0 / 3.0 * (extended[:, 1 : 1 + count] + extended[:, 3 : 3 + count])
    lap = lap - 1.0 / 12.0 * (extended[:, 0:count] + extended[:, 4 : 4 + count])
    for axis in (2, 3):
        lap = lap + 4.0 / 3.0 * (jnp.roll(middle, 1, axis) + jnp.roll(middle, -1, axis))
        lap = lap - 1.0 / 12.0 * (jnp.roll(middle, 2, axis) + jnp.roll(middle, -2, axis))
    return potential[None] * middle - 0.5 * lap


def apply_single(field, potential):
    extended = extended_2(field, (("dom", 1),), 2)
    return stencil(extended, potential)


def filter_single(block, potential):
    previous = block
    current = (apply_single(block, potential) - centre * block) / half
    for step in range(DEGREE - 1):
        following = 2.0 * (apply_single(current, potential) - centre * current) / half - previous
        previous, current = (current, following)
    return current


def body(orbitals, potential):
    block_rows = orbitals.shape[0]
    filtered = orbitals
    filtered = filter_single(filtered, potential)
    flat = filtered.reshape(block_rows, -1).astype(jnp.bfloat16)
    total_cells = float(flat.shape[1] * lax.axis_size("dom"))
    total_orbs = block_rows * lax.axis_size("band")
    my_start = lax.axis_index("band") * block_rows
    every = lax.all_gather(flat, "band", axis=0, tiled=True)
    partial_full = jnp.dot(every, every.T, preferred_element_type=jnp.float32)
    intersection = lax.psum(partial_full, "dom") / total_cells
    lower = jnp.linalg.cholesky(intersection)
    inverse = jax.scipy.linalg.solve_triangular(
        lower, jnp.eye(total_orbs, dtype=jnp.float32), lower=True
    )
    my_rows = lax.dynamic_slice_in_dim(inverse, my_start, block_rows, 0).astype(jnp.bfloat16)
    rotated = jnp.dot(my_rows, every, preferred_element_type=jnp.float32)
    return rotated.reshape(orbitals.shape)


def solution(mesh):
    placed = (P("band", "dom", None, None), P("dom", None, None))
    return jax.shard_map(
        body, mesh=mesh, in_specs=placed, out_specs=P("band", "dom", None, None), check_vma=False
    )
```

profile of v0, /device:TPU:1, one launch (start us, length us, event | category | flops | bytes accessed | tf_op | source)
XLA Modules:
  0.0 533.0 jit_solution(15144045329307927149)
XLA Ops:
  6.5 1.4 fusion.172
  7.9 2.8 collective-permute-start
  10.7 0.6 collective-permute-start.1
  11.3 0.2 fusion.174
  11.8 0.4 fusion.177
  12.2 0.4 fusion.178
  12.5 0.4 fusion.179
  13.0 0.4 copy-done.1
  13.4 0.4 fusion.180
  13.8 3.0 collective-permute-done
  16.8 0.3 constant_dynamic-update-slice_fusion
  17.1 2.5 collective-permute-done.1
  19.6 2.5 broadcast_multiply_fusion
  22.1 0.4 fusion.163
  22.5 0.4 fusion.164
  22.9 0.4 fusion.165
  23.2 0.4 fusion.166
  24.1 10.6 %collective-permute-start.3 = (f32[16,2,32,128]{3,2,1,0:T(8,128)S(1)}, f32[16,2,32,128]{3,2,1,0:T(8,128)S(1)}, u32[]{:S(2)}, u32[]{:S(2)}) collective-permute-start(f32[16,2,32,128]{3,2,1,0:T(8,128)S(1)} %get-tuple-element.96), channel_id=1, source_target_pairs={{1,0},{2,1},{3,2},{4,3},{5,4},{6,5},{7,6},{8,7},{9,8},{10,9},{11,1... | collective-permute-start | bytes 1572872 | tf_op jit(solution)/shard_map/ppermute | solution.py:22
  35.0 1.0 collective-permute-done.2
  36.3 2.6 fusion.73
  38.8 0.4 fusion.154
  39.2 0.4 fusion.155
  39.6 0.4 fusion.156
  40.0 0.4 fusion.157
  40.8 17.2 %collective-permute-start.5 = (f32[16,2,32,128]{3,2,1,0:T(8,128)S(1)}, f32[16,2,32,128]{3,2,1,0:T(8,128)S(1)}, u32[]{:S(2)}, u32[]{:S(2)}) collective-permute-start(f32[16,2,32,128]{3,2,1,0:T(8,128)S(1)} %get-tuple-element.78), channel_id=1, source_target_pairs={{1,0},{2,1},{3,2},{4,3},{5,4},{6,5},{7,6},{8,7},{9,8},{10,9},{11,1... | collective-permute-start | bytes 1572872 | tf_op jit(solution)/shard_map/ppermute | solution.py:22
  58.3 0.9 collective-permute-done.4
  59.2 0.4 collective-permute-done.5
  59.6 2.6 fusion.58
  62.2 0.4 fusion.145
  62.6 0.4 fusion.146
  63.0 0.4 fusion.147
  63.3 0.4 fusion.148
  64.2 16.7 %collective-permute-start.7 = (f32[16,2,32,128]{3,2,1,0:T(8,128)S(1)}, f32[16,2,32,128]{3,2,1,0:T(8,128)S(1)}, u32[]{:S(2)}, u32[]{:S(2)}) collective-permute-start(f32[16,2,32,128]{3,2,1,0:T(8,128)S(1)} %get-tuple-element.60), channel_id=1, source_target_pairs={{1,0},{2,1},{3,2},{4,3},{5,4},{6,5},{7,6},{8,7},{9,8},{10,9},{11,1... | collective-permute-start | bytes 1572872 | tf_op jit(solution)/shard_map/ppermute | solution.py:22
  81.2 1.0 collective-permute-done.6
  82.5 2.6 fusion.43
  85.1 0.4 fusion.136
  85.4 0.4 fusion.137
  85.8 0.4 fusion.138
  86.2 0.4 fusion.139
  87.1 16.9 %collective-permute-start.9 = (f32[16,2,32,128]{3,2,1,0:T(8,128)S(1)}, f32[16,2,32,128]{3,2,1,0:T(8,128)S(1)}, u32[]{:S(2)}, u32[]{:S(2)}) collective-permute-start(f32[16,2,32,128]{3,2,1,0:T(8,128)S(1)} %get-tuple-element.42), channel_id=1, source_target_pairs={{1,0},{2,1},{3,2},{4,3},{5,4},{6,5},{7,6},{8,7},{9,8},{10,9},{11,1... | collective-permute-start | bytes 1572872 | tf_op jit(solution)/shard_map/ppermute | solution.py:22
  104.2 0.8 collective-permute-done.8
  105.1 0.4 collective-permute-done.9
  105.5 2.6 fusion.28
  108.5 0.4 fusion.132
  108.9 0.4 fusion.133
  109.3 0.4 fusion.134
  110.0 16.9 %collective-permute-start.11 = (f32[16,2,32,128]{3,2,1,0:T(8,128)S(1)}, f32[16,2,32,128]{3,2,1,0:T(8,128)S(1)}, u32[]{:S(2)}, u32[]{:S(2)}) collective-permute-start(f32[16,2,32,128]{3,2,1,0:T(8,128)S(1)} %get-tuple-element.8), channel_id=1, source_target_pairs={{1,0},{2,1},{3,2},{4,3},{5,4},{6,5},{7,6},{8,7},{9,8},{10,9},{11,1... | collective-permute-start | bytes 1572872 | tf_op jit(solution)/shard_map/ppermute | solution.py:22
  126.9 0.4 fusion.135
  127.3 0.9 collective-permute-done.10
  128.4 2.6 fusion.120
  131.0 1.1 copy.9
  132.1 0.3 all-reduce.2.cloned.1.call-start
  132.4 108.3 %all-gather.2.cloned.1.call-done = bf16[128,16384]{1,0:T(8,128)(2,1)} async-done(((bf16[16,16384]{1,0:T(8,128)(2,1)}), bf16[128,16384]{1,0:T(8,128)(2,1)}) %all-gather.2.cloned.1.call-update) | async-done | bytes 4194320 | tf_op jit(solution)/shard_map/all_gather | solution.py:63
  240.7 5.3 %fusion.181 = f32[128,128]{0,1:T(8,128)} fusion(bf16[128,16384]{1,0:T(8,128)(2,1)} %all-gather.2.cloned.1.call-done), kind=kOutput, calls=%fused_computation.252 | convolution fusion | flops 536870912 | bytes 4259840 | tf_op jit(solution)/shard_map/dot_general | solution.py:64
  246.1 250.6 %all-reduce.2.cloned.1.call-done = f32[128,128]{0,1:T(8,128)} async-done(((f32[128,128]{0,1:T(8,128)}), f32[128,128]{0,1:T(8,128)}) %all-reduce.2.cloned.1.call-update) | async-done | bytes 65552 | tf_op jit(solution)/shard_map/psum | solution.py:65
  496.7 0.8 broadcast_multiply_fusion.1
  497.7 0.9 fusion.124
  498.5 11.7 %cholesky.17 = f32[128,128]{1,0:T(8,128)S(1)} custom-call(f32[128,128]{1,0:T(8,128)S(1)} %fusion.124), custom_call_target="Cholesky" | custom-call | tf_op jit(solution)/shard_map/jit(cholesky)/cholesky | solution.py:66
  510.3 0.6 compare_reduce_fusion
  510.9 0.7 fusion.121
  511.6 9.8 %custom-call.7 = f32[1,128,128]{1,2,0:T(8,128)S(1)} custom-call(f32[1,128,128]{2,1,0:T(8,128)S(1)} %fusion.121), custom_call_target="InvertDiagBlocksLowerTriangular" | custom-call | tf_op jit(solution)/shard_map/jit(_solve_triangular)/triangular_solve | solution.py:67
  521.4 0.3 fusion.122
  521.7 2.9 convolution_bitcast_fusion
  524.5 1.2 copy.7
  (47 shorter events, 4.9 us)
Async XLA Ops:
  6.5 4.8 copy-start
  6.5 234.2 %all-gather.2.cloned.1.call-start = ((), (), s32[]{:S(2)}) async-start(), calls=%async_computation | async-start | bytes 4718592 | tf_op jit(solution)/shard_map/all_gather | solution.py:63
  7.9 8.9 %collective-permute-start = (f32[16,2,32,128]{3,2,1,0:T(8,128)S(1)}, f32[16,2,32,128]{3,2,1,0:T(8,128)S(1)}, u32[]{:S(2)}, u32[]{:S(2)}) collective-permute-start(f32[16,2,32,128]{3,2,1,0:T(8,128)S(1)} %get-tuple-element.99), channel_id=1, source_target_pairs={{0,1},{1,2},{2,3},{3,4},{4,5},{5,6},{6,7},{7,8},{8,9},{9,10},{10,1... | collective-permute-start | bytes 1572872 | tf_op jit(solution)/shard_map/ppermute | solution.py:20
  10.7 8.9 %collective-permute-start.1 = (f32[16,2,32,128]{3,2,1,0:T(8,128)S(1)}, f32[16,2,32,128]{3,2,1,0:T(8,128)S(1)}, u32[]{:S(2)}, u32[]{:S(2)}) collective-permute-start(f32[16,2,32,128]{3,2,1,0:T(8,128)S(1)} %get-tuple-element.100), channel_id=1, source_target_pairs={{1,0},{2,1},{3,2},{4,3},{5,4},{6,5},{7,6},{8,7},{9,8},{10,9},{11,1... | collective-permute-start | bytes 1572872 | tf_op jit(solution)/shard_map/ppermute | solution.py:22
  12.5 0.8 copy-start.1
  24.0 12.0 %collective-permute-start.2 = (f32[16,2,32,128]{3,2,1,0:T(8,128)S(1)}, f32[16,2,32,128]{3,2,1,0:T(8,128)S(1)}, u32[]{:S(2)}, u32[]{:S(2)}) collective-permute-start(f32[16,2,32,128]{3,2,1,0:T(8,128)S(1)} %get-tuple-element.95), channel_id=1, source_target_pairs={{0,1},{1,2},{2,3},{3,4},{4,5},{5,6},{6,7},{7,8},{8,9},{9,10},{10,1... | collective-permute-start | bytes 1572872 | tf_op jit(solution)/shard_map/ppermute | solution.py:20
  24.1 12.1 %collective-permute-start.3 = (f32[16,2,32,128]{3,2,1,0:T(8,128)S(1)}, f32[16,2,32,128]{3,2,1,0:T(8,128)S(1)}, u32[]{:S(2)}, u32[]{:S(2)}) collective-permute-start(f32[16,2,32,128]{3,2,1,0:T(8,128)S(1)} %get-tuple-element.96), channel_id=1, source_target_pairs={{1,0},{2,1},{3,2},{4,3},{5,4},{6,5},{7,6},{8,7},{9,8},{10,9},{11,1... | collective-permute-start | bytes 1572872 | tf_op jit(solution)/shard_map/ppermute | solution.py:22
  40.7 18.5 %collective-permute-start.4 = (f32[16,2,32,128]{3,2,1,0:T(8,128)S(1)}, f32[16,2,32,128]{3,2,1,0:T(8,128)S(1)}, u32[]{:S(2)}, u32[]{:S(2)}) collective-permute-start(f32[16,2,32,128]{3,2,1,0:T(8,128)S(1)} %get-tuple-element.77), channel_id=1, source_target_pairs={{0,1},{1,2},{2,3},{3,4},{4,5},{5,6},{6,7},{7,8},{8,9},{9,10},{10,1... | collective-permute-start | bytes 1572872 | tf_op jit(solution)/shard_map/ppermute | solution.py:20
  40.8 18.8 %collective-permute-start.5 = (f32[16,2,32,128]{3,2,1,0:T(8,128)S(1)}, f32[16,2,32,128]{3,2,1,0:T(8,128)S(1)}, u32[]{:S(2)}, u32[]{:S(2)}) collective-permute-start(f32[16,2,32,128]{3,2,1,0:T(8,128)S(1)} %get-tuple-element.78), channel_id=1, source_target_pairs={{1,0},{2,1},{3,2},{4,3},{5,4},{6,5},{7,6},{8,7},{9,8},{10,9},{11,1... | collective-permute-start | bytes 1572872 | tf_op jit(solution)/shard_map/ppermute | solution.py:22
  64.1 18.1 %collective-permute-start.6 = (f32[16,2,32,128]{3,2,1,0:T(8,128)S(1)}, f32[16,2,32,128]{3,2,1,0:T(8,128)S(1)}, u32[]{:S(2)}, u32[]{:S(2)}) collective-permute-start(f32[16,2,32,128]{3,2,1,0:T(8,128)S(1)} %get-tuple-element.59), channel_id=1, source_target_pairs={{0,1},{1,2},{2,3},{3,4},{4,5},{5,6},{6,7},{7,8},{8,9},{9,10},{10,1... | collective-permute-start | bytes 1572872 | tf_op jit(solution)/shard_map/ppermute | solution.py:20
  64.2 18.3 %collective-permute-start.7 = (f32[16,2,32,128]{3,2,1,0:T(8,128)S(1)}, f32[16,2,32,128]{3,2,1,0:T(8,128)S(1)}, u32[]{:S(2)}, u32[]{:S(2)}) collective-permute-start(f32[16,2,32,128]{3,2,1,0:T(8,128)S(1)} %get-tuple-element.60), channel_id=1, source_target_pairs={{1,0},{2,1},{3,2},{4,3},{5,4},{6,5},{7,6},{8,7},{9,8},{10,9},{11,1... | collective-permute-start | bytes 1572872 | tf_op jit(solution)/shard_map/ppermute | solution.py:22
  87.0 18.1 %collective-permute-start.8 = (f32[16,2,32,128]{3,2,1,0:T(8,128)S(1)}, f32[16,2,32,128]{3,2,1,0:T(8,128)S(1)}, u32[]{:S(2)}, u32[]{:S(2)}) collective-permute-start(f32[16,2,32,128]{3,2,1,0:T(8,128)S(1)} %get-tuple-element.41), channel_id=1, source_target_pairs={{0,1},{1,2},{2,3},{3,4},{4,5},{5,6},{6,7},{7,8},{8,9},{9,10},{10,1... | collective-permute-start | bytes 1572872 | tf_op jit(solution)/shard_map/ppermute | solution.py:20
  87.1 18.4 %collective-permute-start.9 = (f32[16,2,32,128]{3,2,1,0:T(8,128)S(1)}, f32[16,2,32,128]{3,2,1,0:T(8,128)S(1)}, u32[]{:S(2)}, u32[]{:S(2)}) collective-permute-start(f32[16,2,32,128]{3,2,1,0:T(8,128)S(1)} %get-tuple-element.42), channel_id=1, source_target_pairs={{1,0},{2,1},{3,2},{4,3},{5,4},{6,5},{7,6},{8,7},{9,8},{10,9},{11,1... | collective-permute-start | bytes 1572872 | tf_op jit(solution)/shard_map/ppermute | solution.py:22
  109.9 18.3 %collective-permute-start.10 = (f32[16,2,32,128]{3,2,1,0:T(8,128)S(1)}, f32[16,2,32,128]{3,2,1,0:T(8,128)S(1)}, u32[]{:S(2)}, u32[]{:S(2)}) collective-permute-start(f32[16,2,32,128]{3,2,1,0:T(8,128)S(1)} %get-tuple-element.7), channel_id=1, source_target_pairs={{0,1},{1,2},{2,3},{3,4},{4,5},{5,6},{6,7},{7,8},{8,9},{9,10},{10,1... | collective-permute-start | bytes 1572872 | tf_op jit(solution)/shard_map/ppermute | solution.py:20
  110.0 18.4 %collective-permute-start.11 = (f32[16,2,32,128]{3,2,1,0:T(8,128)S(1)}, f32[16,2,32,128]{3,2,1,0:T(8,128)S(1)}, u32[]{:S(2)}, u32[]{:S(2)}) collective-permute-start(f32[16,2,32,128]{3,2,1,0:T(8,128)S(1)} %get-tuple-element.8), channel_id=1, source_target_pairs={{1,0},{2,1},{3,2},{4,3},{5,4},{6,5},{7,6},{8,7},{9,8},{10,9},{11,1... | collective-permute-start | bytes 1572872 | tf_op jit(solution)/shard_map/ppermute | solution.py:22
  132.1 364.6 %all-reduce.2.cloned.1.call-start = ((), (), s32[]{:S(2)}) async-start(), calls=%async_computation.1 | async-start | bytes 131072 | tf_op jit(solution)/shard_map/psum | solution.py:65
Sparse Core Ops, SparseCore 0:
  132.2 108.4 all-gather.1
  246.2 250.4 all-reduce.1
where the time goes:
time: 542 us; the launch traced here: 533 us
  waiting for transfers between devices  371 us (68%)
  starting transfers between devices  82.4 us (15%)
  other arithmetic  39.9 us (7%)
  local copies, waits for them, and re-layouts  17.2 us (3%)
  between operations  14.4 us (3%)
  matrix products  8.44 us (2%)
    psum x1, waiting for transfers between devices, body(): intersection = lax.psum(partial_full, 'dom') / total_cells  251 us
    all_gather x1, waiting for transfers between devices, body(): every = lax.all_gather(flat, 'band', axis=0, tiled=True)  108 us
    ppermute x6, starting transfers between devices, extended_2(): lax.ppermute(head, axis, [((i + 1) % count, i) for i in range(count)])  79 us
    another operation x3, other arithmetic, body(): lower = jnp.linalg.cholesky(intersection)  12.4 us
  transfers between devices with their start and end apart: 14, of which 14 were waited for; matrix products, arithmetic and copies ran while one was open for 1% of the time, Pallas kernels for 0%

commit v1 on v0

v1 whole, which is shorter than its diff:
```python
import functools

import jax
import jax.numpy as jnp
from jax import lax
from jax.experimental import pallas as pl
from jax.experimental.pallas import tpu as pltpu
from jax.sharding import PartitionSpec as P

MESH = pl.DeviceIdType.MESH
f32, bf16 = jnp.float32, jnp.bfloat16

centre = 5.5
half = 4.5
SCALE = 2.0 / half
DIAGONAL = 0.5 * 7.5 - centre
FIRST = -0.5 * (4.0 / 3.0) * SCALE
SECOND = -1.0 / 16.0

VMEM = pl.BlockSpec(memory_space=pltpu.VMEM)
ANY = pl.BlockSpec(memory_space=pl.ANY)


def remote(src, dst, send_sem, recv_sem, device):
    return pltpu.make_async_remote_copy(
        src_ref=src, dst_ref=dst, send_sem=send_sem, recv_sem=recv_sem, device_id=device, device_id_type=MESH
    )


def wait_bytes(ref, sem):
    pltpu.make_async_copy(ref, ref, sem).wait()


def put(dst, p, o, v):
    dst[p, o, 8:40] = v
    dst[p, o, 0:8] = v[24:32]
    dst[p, o, 40:48] = v[0:8]


def unpack(slot, rec, pot, field):
    for i in range(4):
        pot[4 * slot + i] = (rec[slot, 2, i].astype(f32) + DIAGONAL) * SCALE
        for o in range(2):
            put(field, 4 * slot + i, o, rec[slot, o, i].astype(f32))


def advance(k, first, planes, levels, pot, circulant, sendf):
    src, prev = levels[k - 1], levels[k - 2]
    v = src[pl.ds(first, planes), :, 8:40, :].reshape(planes * 64, 128)
    high = v.astype(bf16)
    low = (v - high.astype(f32)).astype(bf16)
    z = jnp.dot(jnp.concatenate([high, low], axis=1), circulant[...], preferred_element_type=f32)
    for i in range(planes):
        for o in range(2):
            p = first + i
            c = src[p, o, 8:40]
            s1 = src[p - 1, o, 8:40] + src[p + 1, o, 8:40]
            s2 = src[p - 2, o, 8:40] + src[p + 2, o, 8:40]
            s1 = s1 + (src[p, o, 7:39] + src[p, o, 9:41])
            s2 = s2 + (src[p, o, 6:38] + src[p, o, 10:42])
            at = (i * 2 + o) * 32
            w = pot[p] * c + (s1 + z[at : at + 32] + s2 * SECOND) * FIRST
            w = w * 0.5 if k == 1 else w - prev[p, o, 8:40]
            if k < 6:
                put(levels[k], p, o, w)
            else:
                w = w.astype(bf16)
                sendf[2 * (p - 12), o] = w[0:16]
                sendf[2 * (p - 12) + 1, o] = w[16:32]


def filter_kernel(
    orb_hbm, pot_hbm, t_ref, gram_ref,
    orb, potv, send, rec, pot, circulant, sendf, gath, part, r1, q1, r2, q2, r3, q3, *rest
):
    levels, (lsem, ssem, rsem, fsem, gsem, asem) = rest[:6], rest[6:]
    b, d = lax.axis_index("band"), lax.axis_index("dom")
    yc, zh = d % 8, d // 8
    me = yc * 8 + b

    load = pltpu.make_async_copy(orb_hbm, orb, lsem.at[0])
    load.start()
    loadp = pltpu.make_async_copy(pot_hbm, potv, lsem.at[1])
    loadp.start()

    barrier = pltpu.get_barrier_semaphore()

    @pl.loop(1, 64)
    def _(i):
        q = (me + i) % 64
        pl.semaphore_signal(barrier, inc=1, device_id=(q % 8, zh * 8 + q // 8), device_id_type=MESH)

    for i in range(1, 4):
        pl.semaphore_signal(barrier, inc=1, device_id=(b, (zh + i) % 4 * 8 + yc), device_id_type=MESH)

    r = lax.broadcasted_iota(jnp.int32, (128, 128), 0)
    c = lax.broadcasted_iota(jnp.int32, (128, 128), 1)
    apart = (r - c + 128) % 128
    near = jnp.where((apart == 1) | (apart == 127), 1.0, 0.0)
    far = jnp.where((apart == 2) | (apart == 126), SECOND, 0.0)
    for h in range(2):
        circulant[h * 128 : (h + 1) * 128] = (near + far).astype(bf16)

    load.wait()
    loadp.wait()

    @pl.loop(0, 8)
    def _(k):
        for i in range(4):
            for o in range(2):
                send[k, o, i] = orb[2 * k + o, i].astype(bf16)
            send[k, 2, i] = potv[i].astype(bf16)

    rec[3 + yc] = send[yc]
    pl.semaphore_wait(barrier, 66)

    def out_copy(i):
        k = (yc + i) % 8
        return remote(send.at[k], rec.at[3 + yc], ssem.at[i], rsem.at[3 + yc], (b, zh * 8 + k))

    def in_copy(k):
        return remote(send.at[k], rec.at[3 + k], ssem.at[0], rsem.at[3 + k], (b, zh * 8 + k))

    def down(k):
        return remote(rec.at[3 + k], rec.at[11 + k], fsem.at[k], rsem.at[11 + k], (b, (zh + 3) % 4 * 8 + yc))

    def up(k):
        return remote(rec.at[3 + k], rec.at[k - 5], fsem.at[k], rsem.at[k - 5], (b, (zh + 1) % 4 * 8 + yc))

    def forward(k):
        @pl.when(k < 3)
        def _():
            down(k).start()

        @pl.when(k >= 5)
        def _():
            up(k).start()

    for i in range(1, 8):
        out_copy(i).start()
    forward(yc)
    unpack(3 + yc, rec, pot, levels[0])

    @pl.loop(1, 8)
    def _(i):
        k = (yc + 8 - i) % 8
        in_copy(k).wait_recv()
        forward(k)
        unpack(3 + k, rec, pot, levels[0])

    step = functools.partial(advance, levels=levels, pot=pot, circulant=circulant, sendf=sendf)
    for k in range(1, 7):
        planes = (32 - 4 * k) // 2

        @pl.loop(0, 2)
        def _(t):
            step(k, 12 + 2 * k + planes * t, planes)

    for s in range(3):
        up(5 + s).wait_recv()
        down(s).wait_recv()

    @pl.loop(0, 3)
    def _(s):
        unpack(s, rec, pot, levels[0])
        unpack(11 + s, rec, pot, levels[0])

    for k in range(1, 7):

        @pl.loop(0, 2)
        def _(t):
            step(k, 2 * k + t * (44 - 4 * k), 12)

    own = pl.ds(b * 16 + yc * 2, 2)
    gath[own] = sendf[me]

    @pl.loop(1, 64)
    def _(i):
        q = (me + i) % 64
        remote(sendf.at[q], gath.at[own], gsem.at[0], gsem.at[1], (q % 8, zh * 8 + q // 8)).start()

    for i in range(1, 8):
        out_copy(i).wait_send()
    for k in (0, 1, 2):
        down(k).wait_send()
    for k in (5, 6, 7):
        up(k).wait_send()
    wait_bytes(gath.at[0:126], gsem.at[1])

    t = jnp.swapaxes(gath[...].astype(f32), 0, 1).astype(bf16)
    t_ref[...] = t
    x = jnp.concatenate([t[j] for j in range(16)], axis=1)
    gram = lax.dot_general(x, x, (((1,), (1,)), ((), ())), preferred_element_type=f32)
    part[...] = gram.reshape(8, 16, 128)
    r1[yc] = part[yc]
    for i in range(1, 8):
        k = (yc + i) % 8
        remote(part.at[k], r1.at[yc], asem.at[0], asem.at[1], (b, zh * 8 + k)).start()
    wait_bytes(r1.at[0:7], asem.at[1])
    q1[...] = jnp.sum(r1[...], axis=0)
    r2[b] = q1[...]
    for i in range(1, 8):
        remote(q1, r2.at[b], asem.at[2], asem.at[3], ((b + i) % 8, d)).start()
    wait_bytes(r2.at[0:7], asem.at[3])
    q2[...] = jnp.sum(r2[...], axis=0)
    r3[zh] = q2[...]
    for i in range(1, 4):
        remote(q2, r3.at[zh], asem.at[4], asem.at[5], (b, (zh + i) % 4 * 8 + yc)).start()
    wait_bytes(r3.at[0:3], asem.at[5])
    q3[...] = jnp.sum(r3[...], axis=0)
    gram_ref[yc] = q3[...]
    for i in range(1, 8):
        remote(q3, gram_ref.at[yc], asem.at[6], asem.at[7], (b, zh * 8 + (yc + i) % 8)).start()
    wait_bytes(gram_ref.at[0:7], asem.at[7])
    wait_bytes(gath.at[0:126], gsem.at[0])
    wait_bytes(r1.at[0:7], asem.at[0])
    wait_bytes(r2.at[0:7], asem.at[2])
    wait_bytes(r3.at[0:3], asem.at[4])
    wait_bytes(r1.at[0:7], asem.at[6])


def rotate_kernel(w_ref, t_ref, out_ref, sendr, recr, ssem, rsem):
    b, d = lax.axis_index("band"), lax.axis_index("dom")
    barrier = pltpu.get_barrier_semaphore()
    for i in range(1, 8):
        pl.semaphore_signal(barrier, inc=1, device_id=((b + i) % 8, d), device_id_type=MESH)
    for j in range(16):
        rows = jnp.dot(w_ref[...], t_ref[j], preferred_element_type=f32).astype(bf16)
        for k in range(8):
            sendr[k, j] = rows[16 * k : 16 * k + 16]
    recr[b] = sendr[b]
    pl.semaphore_wait(barrier, 7)

    def out_copy(i):
        k = (b + i) % 8
        return remote(sendr.at[k], recr.at[b], ssem.at[i], rsem.at[b], (k, d))

    for i in range(1, 8):
        out_copy(i).start()

    def place(k):
        block = jnp.swapaxes(recr[k].astype(f32), 0, 1)
        out_ref[:, k // 2, pl.ds(pl.multiple_of(k % 2 * 16, 16), 16), :] = block

    place(b)

    @pl.loop(1, 8)
    def _(i):
        k = (b + 8 - i) % 8
        remote(sendr.at[k], recr.at[k], ssem.at[0], rsem.at[k], (k, d)).wait_recv()
        place(k)

    for i in range(1, 8):
        out_copy(i).wait_send()


def body(orbitals, potential):
    dma = pltpu.SemaphoreType.DMA
    t, gram = pl.pallas_call(
        filter_kernel,
        out_shape=(jax.ShapeDtypeStruct((16, 128, 128), bf16), jax.ShapeDtypeStruct((8, 16, 128), f32)),
        in_specs=[ANY, ANY],
        out_specs=(VMEM, VMEM),
        scratch_shapes=[
            pltpu.VMEM((16, 4, 32, 128), f32),
            pltpu.VMEM((4, 32, 128), f32),
            pltpu.VMEM((8, 3, 4, 32, 128), bf16),
            pltpu.VMEM((14, 3, 4, 32, 128), bf16),
            pltpu.VMEM((56, 32, 128), f32),
            pltpu.VMEM((256, 128), bf16),
            pltpu.VMEM((64, 2, 16, 128), bf16),
            pltpu.VMEM((128, 16, 128), bf16),
            pltpu.VMEM((8, 16, 128), f32),
            pltpu.VMEM((8, 16, 128), f32),
            pltpu.VMEM((16, 128), f32),
            pltpu.VMEM((8, 16, 128), f32),
            pltpu.VMEM((16, 128), f32),
            pltpu.VMEM((4, 16, 128), f32),
            pltpu.VMEM((16, 128), f32),
        ]
        + [pltpu.VMEM((56, 2, 48, 128), f32)] * 6
        + [dma((2,)), dma((8,)), dma((14,)), dma((8,)), dma((2,)), dma((8,))],
        compiler_params=pltpu.CompilerParams(collective_id=0, has_side_effects=True, vmem_limit_bytes=52 << 20),
    )(orbitals, potential)
    total_cells = 2048.0 * 256.0
    intersection = gram.reshape(128, 128) / total_cells
    lower = jnp.linalg.cholesky(intersection)
    inverse = jax.scipy.linalg.solve_triangular(lower, jnp.eye(128, dtype=f32), lower=True).astype(bf16)
    return pl.pallas_call(
        rotate_kernel,
        out_shape=jax.ShapeDtypeStruct((16, 4, 32, 128), f32),
        in_specs=[VMEM, VMEM],
        out_specs=VMEM,
        scratch_shapes=[
            pltpu.VMEM((8, 16, 16, 128), bf16),
            pltpu.VMEM((8, 16, 16, 128), bf16),
            dma((8,)),
            dma((8,)),
        ],
        compiler_params=pltpu.CompilerParams(collective_id=1, has_side_effects=True, vmem_limit_bytes=24 << 20),
    )(inverse, t)


def solution(mesh):
    placed = (P("band", "dom", None, None), P("dom", None, None))
    return jax.shard_map(
        body, mesh=mesh, in_specs=placed, out_specs=P("band", "dom", None, None), check_vma=False
    )
```

time: 542 us -> 102 us (0.19); the launches traced: 533 us -> 102 us
  waiting for transfers between devices: 371 us -> 0 us
  starting transfers between devices: 82.4 us -> 0 us
  Pallas kernels: 0 us -> 75.8 us
  other arithmetic: 39.9 us -> 22.9 us
  between operations: 14.4 us -> 0.06 us
  local copies, waits for them, and re-layouts: 17.2 us -> 3.12 us
  matrix products: 8.44 us -> 0.25 us
    psum x1 -> x0, waiting for transfers between devices: 251 us -> none  [body(): intersection = lax.psum(partial_full, 'dom') / total_cells]
    all_gather x1 -> x0, waiting for transfers between devices: 108 us -> none  [body(): every = lax.all_gather(flat, 'band', axis=0, tiled=True)]
    ppermute x12 -> x0, starting transfers between devices: 82.2 us -> none  [the longest x6 79 us: extended_2(): lax.ppermute(head, axis, [((i + 1) % count, i) for i in range(count)])]
    pallas_call x0 -> x2, Pallas kernels: none -> 75.8 us  [the longest x1 64.6 us: body(): pl.pallas_call(filter_kernel, out_shape=(jax.ShapeDtypeStruct((16, 128, 1...]
    slice x54 -> x0, local copies, waits for them, and re-layouts: 14 us -> none  [the longest x16 4.06 us: stencil(): jnp.roll(middle, -2, axis)]
    ppermute x12 -> x0, waiting for transfers between devices: 11.6 us -> none  [the longest x6 7.66 us: extended_2(): lax.ppermute(tail, axis, [(i, (i + 1) % count) for i in range(count)])]
    sub x4 -> x0, other arithmetic: 10.3 us -> none  [filter_single(): 2.0 * (apply_single(current, potential) - centre * current) / half]
    dot_general x2 -> x0, matrix products: 8.19 us -> none  [the longest x1 5.34 us: body(): partial_full = jnp.dot(every, every.T, preferred_element_type=jnp.float32)]
  transfers between devices with their start and end apart: 14 -> 0, of which waited for: 14 -> 0; matrix products, arithmetic and copies ran while one was open for 1% -> 0% of each run, Pallas kernels for 0% -> 0%
where the time goes in v1:
time: 102 us
  Pallas kernels  75.8 us (74%)
  other arithmetic  22.9 us (22%)
  local copies, waits for them, and re-layouts  3.12 us (3%)
    pallas_call x1, Pallas kernels, body(): pl.pallas_call(filter_kernel, out_shape=(jax.ShapeDtypeStruct((16, 128, 1...  64.6 us
    another operation x3, other arithmetic, body(): lower = jnp.linalg.cholesky(intersection)  12.4 us
    pallas_call x1, Pallas kernels, body(): pl.pallas_call(rotate_kernel, out_shape=jax.ShapeDtypeStruct((16, 4, 32,...  11.3 us
    another operation x2, other arithmetic, body(): jax.scipy.linalg.solve_triangular(lower, jnp.eye(128, dtype=f32), lower=T...  10.5 us
    unnamed x5, local copies, waits for them, and re-layouts  3.04 us

profile of v1, /device:TPU:1, one launch (start us, length us, event | category | flops | bytes accessed | tf_op | source)
XLA Modules:
  0.0 102.1 jit_solution(11735956130860763007)
XLA Ops:
  0.0 0.0 copy-start
  0.0 1.2 %copy-done = f32[16,4,32,128]{3,2,1,0:T(8,128)S(1)} copy-done((f32[16,4,32,128]{3,2,1,0:T(8,128)S(1)}, f32[16,4,32,128]{3,2,1,0:T(8,128)}, u32[]{:S(2)}) %copy-start) | copy-done | bytes 1048600
  1.2 0.0 copy-start.1
  1.2 0.8 copy-done.1
  2.1 64.6 %shard_map.28 = (bf16[16,128,128]{2,1,0:T(8,128)(2,1)S(1)}, f32[8,16,128]{2,1,0:T(8,128)S(1)}) custom-call(f32[16,4,32,128]{3,2,1,0:T(8,128)S(1)} %copy-done, f32[4,32,128]{2,1,0:T(8,128)S(1)} %copy-done.1), custom_call_target="tpu_custom_call" | custom-call | tf_op jit(solution)/shard_map/pallas_call | solution.py:259
  66.6 0.1 copy.5
  66.8 11.7 %cholesky.17 = f32[128,128]{1,0:T(8,128)S(1)} custom-call(f32[128,128]{1,0:T(8,128)S(1)} %fusion.2), custom_call_target="Cholesky" | custom-call | tf_op jit(solution)/shard_map/jit(cholesky)/cholesky | solution.py:287
  78.5 0.6 compare_reduce_fusion
  79.2 0.7 fusion
  79.8 9.8 %custom-call.7 = f32[1,128,128]{1,2,0:T(8,128)S(1)} custom-call(f32[1,128,128]{2,1,0:T(8,128)S(1)} %fusion), custom_call_target="InvertDiagBlocksLowerTriangular" | custom-call | tf_op jit(solution)/shard_map/jit(_solve_triangular)/triangular_solve | solution.py:288
  89.6 0.3 convolution_convert_fusion.w_ref
  89.9 11.3 %shard_map.29 = f32[16,4,32,128]{3,2,1,0:T(8,128)S(1)} custom-call(bf16[128,128]{1,0:T(8,128)(2,1)S(1)} %convolution_convert_fusion.w_ref, bf16[16,128,128]{2,1,0:T(8,128)(2,1)S(1)} %get-tuple-element.8.t_ref), custom_call_target="tpu_custom_call" | custom-call | tf_op jit(solution)/shard_map/pallas_call | solution.py:289
  101.2 1.0 copy.7
  (3 shorter events, 0.1 us)
Async XLA Ops:
  0.0 1.2 %copy-start = (f32[16,4,32,128]{3,2,1,0:T(8,128)S(1)}, f32[16,4,32,128]{3,2,1,0:T(8,128)}, u32[]{:S(2)}) copy-start(f32[16,4,32,128]{3,2,1,0:T(8,128)} %orb_hbm.1) | copy-start | bytes 3145732
  1.2 0.8 copy-start.1

commit v2 on v1

--- a/solution.py
+++ b/solution.py
@@ -69,11 +69,46 @@
                 sendf[2 * (p - 12) + 1, o] = w[16:32]
 
 
-def filter_kernel(
-    orb_hbm, pot_hbm, t_ref, gram_ref,
-    orb, potv, send, rec, pot, circulant, sendf, gath, part, r1, q1, r2, q2, r3, q3, *rest
+def inverse_factor(m):
+    n, nb = 128, 16
+    row = lax.broadcasted_iota(jnp.int32, (nb, n), 0)
+    lane = lax.broadcasted_iota(jnp.int32, (nb, n), 1)
+    out = []
+    for k in range(n // nb):
+        at, lo = k * nb, (k + 1) * nb
+        x = m[at:lo]
+        cols = [jnp.broadcast_to(x[:, at + t : at + t + 1], (nb, n)) for t in range(nb)]
+        own = (lane >= at) & (lane < lo)
+        x = jnp.where(own, jnp.where(lane - at == row, 1.0, 0.0), x)
+        w = jnp.zeros_like(x)
+        for t in range(nb):
+            here = row == t
+            pivot = jnp.broadcast_to(cols[t][t : t + 1], (nb, n))
+            inv = 1.0 / pivot
+            r = jnp.broadcast_to(x[t : t + 1], (nb, n))
+            w = jnp.where(here, r * lax.rsqrt(pivot), w)
+            mult = jnp.where(here, 1.0 - inv, cols[t] * inv)
+            x = x - mult * r
+            for u in range(t + 1, nb):
+                cols[u] = cols[u] - mult * jnp.broadcast_to(cols[u][t : t + 1], (nb, n))
+        out.append(jnp.where(lane < lo, w, 0.0))
+        if lo < n:
+            below = m[lo:]
+            lane_b = lax.broadcasted_iota(jnp.int32, below.shape, 1)
+            padded = [jnp.zeros((at, n), f32)] * (at > 0) + [x, jnp.zeros((n - lo, n), f32)]
+            change = jnp.dot(
+                below, jnp.concatenate(padded, 0), precision=lax.Precision.HIGHEST, preferred_element_type=f32
+            )
+            kept = jnp.where((lane_b >= at) & (lane_b < lo), 0.0, below)
+            m = jnp.concatenate([m[:lo], kept - change], axis=0)
+    return out
+
+
+def kernel(
+    orb_hbm, pot_hbm, out_hbm,
+    orb, potv, send, rec, pot, circulant, sendf, gath, part, r1, q1, r2, q2, r3, q3, gram_ref, t_ref, sendr, recr, outv, *rest
 ):
-    levels, (lsem, ssem, rsem, fsem, gsem, asem) = rest[:6], rest[6:]
+    levels, (lsem, ssem, rsem, fsem, gsem, asem, bsem, csem, osem) = rest[:6], rest[6:]
     b, d = lax.axis_index("band"), lax.axis_index("dom")
     yc, zh = d % 8, d // 8
     me = yc * 8 + b
@@ -212,55 +247,57 @@
     for i in range(1, 8):
         remote(q3, gram_ref.at[yc], asem.at[6], asem.at[7], (b, zh * 8 + (yc + i) % 8)).start()
     wait_bytes(gram_ref.at[0:7], asem.at[7])
+
+    inverse = inverse_factor(gram_ref[...].reshape(128, 128) * (1.0 / 2.0**19))
+    w = jnp.concatenate([block.astype(bf16) for block in inverse], axis=0)
+    for j in range(16):
+        rows = jnp.dot(w, t_ref[j], preferred_element_type=f32).astype(bf16)
+        for k in range(8):
+            sendr[k, j] = rows[16 * k : 16 * k + 16]
+
+    def back_copy(i):
+        k = (b + i) % 8
+        return remote(sendr.at[k], recr.at[b], bsem.at[i], csem.at[b], (k, d))
+
+    def place_copy(k):
+        rows = pl.ds(pl.multiple_of(k % 2 * 16, 16), 16)
+        return pltpu.make_async_copy(outv.at[k], out_hbm.at[:, k // 2, rows, :], osem.at[k])
+
+    def place(k):
+        outv[k] = jnp.swapaxes(recr[k].astype(f32), 0, 1)
+        place_copy(k).start()
+
+    for i in range(1, 8):
+        back_copy(i).start()
+    recr[b] = sendr[b]
+    place(b)
+
+    @pl.loop(1, 8)
+    def _(i):
+        k = (b + 8 - i) % 8
+        remote(sendr.at[k], recr.at[k], bsem.at[0], csem.at[k], (k, d)).wait_recv()
+        place(k)
+
     wait_bytes(gath.at[0:126], gsem.at[0])
     wait_bytes(r1.at[0:7], asem.at[0])
     wait_bytes(r2.at[0:7], asem.at[2])
     wait_bytes(r3.at[0:3], asem.at[4])
     wait_bytes(r1.at[0:7], asem.at[6])
-
-
-def rotate_kernel(w_ref, t_ref, out_ref, sendr, recr, ssem, rsem):
-    b, d = lax.axis_index("band"), lax.axis_index("dom")
-    barrier = pltpu.get_barrier_semaphore()
-    for i in range(1, 8):
-        pl.semaphore_signal(barrier, inc=1, device_id=((b + i) % 8, d), device_id_type=MESH)
-    for j in range(16):
-        rows = jnp.dot(w_ref[...], t_ref[j], preferred_element_type=f32).astype(bf16)
-        for k in range(8):
-            sendr[k, j] = rows[16 * k : 16 * k + 16]
-    recr[b] = sendr[b]
-    pl.semaphore_wait(barrier, 7)
-
-    def out_copy(i):
-        k = (b + i) % 8
-        return remote(sendr.at[k], recr.at[b], ssem.at[i], rsem.at[b], (k, d))
-
-    for i in range(1, 8):
-        out_copy(i).start()
-
-    def place(k):
-        block = jnp.swapaxes(recr[k].astype(f32), 0, 1)
-        out_ref[:, k // 2, pl.ds(pl.multiple_of(k % 2 * 16, 16), 16), :] = block
-
-    place(b)
-
-    @pl.loop(1, 8)
-    def _(i):
-        k = (b + 8 - i) % 8
-        remote(sendr.at[k], recr.at[k], ssem.at[0], rsem.at[k], (k, d)).wait_recv()
-        place(k)
-
-    for i in range(1, 8):
-        out_copy(i).wait_send()
+    for i in range(1, 8):
+        back_copy(i).wait_send()
+
+    @pl.loop(0, 8)
+    def _(k):
+        place_copy(k).wait()
 
 
 def body(orbitals, potential):
     dma = pltpu.SemaphoreType.DMA
-    t, gram = pl.pallas_call(
-        filter_kernel,
-        out_shape=(jax.ShapeDtypeStruct((16, 128, 128), bf16), jax.ShapeDtypeStruct((8, 16, 128), f32)),
+    return pl.pallas_call(
+        kernel,
+        out_shape=jax.ShapeDtypeStruct((16, 4, 32, 128), f32),
         in_specs=[ANY, ANY],
-        out_specs=(VMEM, VMEM),
+        out_specs=ANY,
         scratch_shapes=[
             pltpu.VMEM((16, 4, 32, 128), f32),
             pltpu.VMEM((4, 32, 128), f32),
@@ -277,28 +314,16 @@
             pltpu.VMEM((16, 128), f32),
             pltpu.VMEM((4, 16, 128), f32),
             pltpu.VMEM((16, 128), f32),
+            pltpu.VMEM((8, 16, 128), f32),
+            pltpu.VMEM((16, 128, 128), bf16),
+            pltpu.VMEM((8, 16, 16, 128), bf16),
+            pltpu.VMEM((8, 16, 16, 128), bf16),
+            pltpu.VMEM((8, 16, 16, 128), f32),
         ]
         + [pltpu.VMEM((56, 2, 48, 128), f32)] * 6
-        + [dma((2,)), dma((8,)), dma((14,)), dma((8,)), dma((2,)), dma((8,))],
-        compiler_params=pltpu.CompilerParams(collective_id=0, has_side_effects=True, vmem_limit_bytes=52 << 20),
+        + [dma((2,)), dma((8,)), dma((14,)), dma((8,)), dma((2,)), dma((8,)), dma((8,)), dma((8,)), dma((8,))],
+        compiler_params=pltpu.CompilerParams(collective_id=0, has_side_effects=True, vmem_limit_bytes=60 << 20),
     )(orbitals, potential)
-    total_cells = 2048.0 * 256.0
-    intersection = gram.reshape(128, 128) / total_cells
-    lower = jnp.linalg.cholesky(intersection)
-    inverse = jax.scipy.linalg.solve_triangular(lower, jnp.eye(128, dtype=f32), lower=True).astype(bf16)
-    return pl.pallas_call(
-        rotate_kernel,
-        out_shape=jax.ShapeDtypeStruct((16, 4, 32, 128), f32),
-        in_specs=[VMEM, VMEM],
-        out_specs=VMEM,
-        scratch_shapes=[
-            pltpu.VMEM((8, 16, 16, 128), bf16),
-            pltpu.VMEM((8, 16, 16, 128), bf16),
-            dma((8,)),
-            dma((8,)),
-        ],
-        compiler_params=pltpu.CompilerParams(collective_id=1, has_side_effects=True, vmem_limit_bytes=24 << 20),
-    )(inverse, t)
 
 
 def solution(mesh):

time: 102 us -> 79.3 us (0.78)
  other arithmetic: 22.9 us -> 0 us
  Pallas kernels: 75.8 us -> 76.9 us
    another operation x5 -> x0, other arithmetic: 22.9 us -> none  [the longest x3 12.4 us: body(): lower = jnp.linalg.cholesky(intersection)]
    pallas_call x2 -> x1, Pallas kernels: 75.8 us -> 76.9 us  [body(): pl.pallas_call(kernel, out_shape=jax.ShapeDtypeStruct((16, 4, 32, 128), f...]
    unnamed x5 -> x1, local copies, waits for them, and re-layouts: 3.04 us -> 2.29 us
where the time goes in v2:
time: 79.3 us; the launch traced here: 79.2 us
  Pallas kernels  76.9 us (97%)
  local copies, waits for them, and re-layouts  2.29 us (3%)
    pallas_call x1, Pallas kernels, body(): pl.pallas_call(kernel, out_shape=jax.ShapeDtypeStruct((16, 4, 32, 128), f...  76.9 us
    unnamed x1, local copies, waits for them, and re-layouts  2.29 us

profile of v2, /device:TPU:1, one launch (start us, length us, event | category | flops | bytes accessed | tf_op | source)
XLA Modules:
  0.0 79.2 jit_solution(5935869594765533994)
XLA Ops:
  0.0 76.9 %shard_map.28 = f32[16,4,32,128]{3,2,1,0:T(8,128)} custom-call(f32[16,4,32,128]{3,2,1,0:T(8,128)} %orb_hbm.1, f32[4,32,128]{2,1,0:T(8,128)} %pot_hbm.1), custom_call_target="tpu_custom_call" | custom-call | tf_op jit(solution)/shard_map/pallas_call | solution.py:296
  76.9 2.3 %copy.4 = f32[16,4,32,128]{3,2,1,0:T(8,128)} copy(f32[16,4,32,128]{3,2,1,0:T(8,128)} %shard_map.28) | data formatting | bytes 2097152

commit v3 on v2

--- a/solution.py
+++ b/solution.py
@@ -37,36 +37,40 @@
     dst[p, o, 40:48] = v[0:8]
 
 
-def unpack(slot, rec, pot, field):
+def unpack(slot, rec, field):
     for i in range(4):
-        pot[4 * slot + i] = (rec[slot, 2, i].astype(f32) + DIAGONAL) * SCALE
         for o in range(2):
             put(field, 4 * slot + i, o, rec[slot, o, i].astype(f32))
 
 
-def advance(k, first, planes, levels, pot, circulant, sendf):
+def scaled(plane):
+    return (plane.astype(f32) + DIAGONAL) * SCALE
+
+
+def advance(k, segments, levels, pot, circulant, sendf):
     src, prev = levels[k - 1], levels[k - 2]
-    v = src[pl.ds(first, planes), :, 8:40, :].reshape(planes * 64, 128)
-    high = v.astype(bf16)
-    low = (v - high.astype(f32)).astype(bf16)
-    z = jnp.dot(jnp.concatenate([high, low], axis=1), circulant[...], preferred_element_type=f32)
-    for i in range(planes):
-        for o in range(2):
-            p = first + i
-            c = src[p, o, 8:40]
-            s1 = src[p - 1, o, 8:40] + src[p + 1, o, 8:40]
-            s2 = src[p - 2, o, 8:40] + src[p + 2, o, 8:40]
-            s1 = s1 + (src[p, o, 7:39] + src[p, o, 9:41])
-            s2 = s2 + (src[p, o, 6:38] + src[p, o, 10:42])
-            at = (i * 2 + o) * 32
-            w = pot[p] * c + (s1 + z[at : at + 32] + s2 * SECOND) * FIRST
-            w = w * 0.5 if k == 1 else w - prev[p, o, 8:40]
-            if k < 6:
-                put(levels[k], p, o, w)
-            else:
-                w = w.astype(bf16)
-                sendf[2 * (p - 12), o] = w[0:16]
-                sendf[2 * (p - 12) + 1, o] = w[16:32]
+    for first, planes in segments:
+        v = src[pl.ds(first, planes), :, 8:40, :].reshape(planes * 64, 128)
+        high = v.astype(bf16)
+        low = (v - high.astype(f32)).astype(bf16)
+        z = jnp.dot(jnp.concatenate([high, low], axis=1), circulant[...], preferred_element_type=f32)
+        for i in range(planes):
+            for o in range(2):
+                p = first + i
+                c = src[p, o, 8:40]
+                s1 = src[p - 1, o, 8:40] + src[p + 1, o, 8:40]
+                s2 = src[p - 2, o, 8:40] + src[p + 2, o, 8:40]
+                s1 = s1 + (src[p, o, 7:39] + src[p, o, 9:41])
+                s2 = s2 + (src[p, o, 6:38] + src[p, o, 10:42])
+                at = (i * 2 + o) * 32
+                w = pot[p] * c + (s1 + z[at : at + 32] + s2 * SECOND) * FIRST
+                w = w * 0.5 if k == 1 else w - prev[p, o, 8:40]
+                if k < 6:
+                    put(levels[k], p, o, w)
+                else:
+                    w = w.astype(bf16)
+                    sendf[2 * (p - 12), o] = w[0:16]
+                    sendf[2 * (p - 12) + 1, o] = w[16:32]
 
 
 def inverse_factor(m):
@@ -106,27 +110,37 @@
 
 def kernel(
     orb_hbm, pot_hbm, out_hbm,
-    orb, potv, send, rec, pot, circulant, sendf, gath, part, r1, q1, r2, q2, r3, q3, gram_ref, t_ref, sendr, recr, outv, *rest
+    orb, potv, potb, potp, poth, potg, poti, send, rec, pot, circulant, sendf, gath,
+    part, r1, q1, r2, q2, r3, q3, gram_ref, t_ref, sendr, recr, outv, *rest
 ):
-    levels, (lsem, ssem, rsem, fsem, gsem, asem, bsem, csem, osem) = rest[:6], rest[6:]
+    levels, (lsem, psem, ssem, rsem, fsem, gsem, asem, bsem, csem, osem) = rest[:6], rest[6:]
     b, d = lax.axis_index("band"), lax.axis_index("dom")
     yc, zh = d % 8, d // 8
+    x, lower = b // 2, b % 2
     me = yc * 8 + b
-
+    above, below = (zh + 1) % 4 * 8, (zh + 3) % 4 * 8
+
+    loadp = pltpu.make_async_copy(pot_hbm, potv, lsem.at[1])
+    loadp.start()
     load = pltpu.make_async_copy(orb_hbm, orb, lsem.at[0])
     load.start()
-    loadp = pltpu.make_async_copy(pot_hbm, potv, lsem.at[1])
-    loadp.start()
 
     barrier = pltpu.get_barrier_semaphore()
+
+    def greet(device):
+        pl.semaphore_signal(barrier, inc=1, device_id=device, device_id_type=MESH)
 
     @pl.loop(1, 64)
     def _(i):
         q = (me + i) % 64
-        pl.semaphore_signal(barrier, inc=1, device_id=(q % 8, zh * 8 + q // 8), device_id_type=MESH)
-
-    for i in range(1, 4):
-        pl.semaphore_signal(barrier, inc=1, device_id=(b, (zh + i) % 4 * 8 + yc), device_id_type=MESH)
+        greet((q % 8, zh * 8 + q // 8))
+
+    @pl.loop(0, 8)
+    def _(k):
+        greet((b, above + k))
+        greet((b, below + k))
+
+    greet((b, (zh + 2) % 4 * 8 + yc))
 
     r = lax.broadcasted_iota(jnp.int32, (128, 128), 0)
     c = lax.broadcasted_iota(jnp.int32, (128, 128), 1)
@@ -136,52 +150,80 @@
     for h in range(2):
         circulant[h * 128 : (h + 1) * 128] = (near + far).astype(bf16)
 
+    loadp.wait()
+    potb[...] = potv[...].astype(bf16)
+    potp[yc] = potb[x]
+    pl.semaphore_wait(barrier, 80)
+
+    for i in range(1, 8):
+        remote(potb.at[x], potp.at[yc], psem.at[0], psem.at[1], (b, zh * 8 + (yc + i) % 8)).start()
+
+    @pl.when(yc < 3)
+    def _():
+        for k in range(8):
+            remote(potb.at[x], poth.at[3 + yc], psem.at[2], psem.at[3], (b, below + k)).start()
+
+    @pl.when(yc >= 5)
+    def _():
+        for k in range(8):
+            remote(potb.at[x], poth.at[yc - 5], psem.at[2], psem.at[3], (b, above + k)).start()
+
     load.wait()
-    loadp.wait()
-
-    @pl.loop(0, 8)
-    def _(k):
-        for i in range(4):
-            for o in range(2):
-                send[k, o, i] = orb[2 * k + o, i].astype(bf16)
-            send[k, 2, i] = potv[i].astype(bf16)
-
-    rec[3 + yc] = send[yc]
-    pl.semaphore_wait(barrier, 66)
-
-    def out_copy(i):
-        k = (yc + i) % 8
-        return remote(send.at[k], rec.at[3 + yc], ssem.at[i], rsem.at[3 + yc], (b, zh * 8 + k))
+
+    def out_copy(k):
+        return remote(send.at[k], rec.at[3 + yc], ssem.at[k], rsem.at[3 + yc], (b, zh * 8 + k))
 
     def in_copy(k):
         return remote(send.at[k], rec.at[3 + k], ssem.at[0], rsem.at[3 + k], (b, zh * 8 + k))
 
     def down(k):
-        return remote(rec.at[3 + k], rec.at[11 + k], fsem.at[k], rsem.at[11 + k], (b, (zh + 3) % 4 * 8 + yc))
+        return remote(rec.at[3 + k], rec.at[11 + k], fsem.at[k], rsem.at[11 + k], (b, below + yc))
 
     def up(k):
-        return remote(rec.at[3 + k], rec.at[k - 5], fsem.at[k], rsem.at[k - 5], (b, (zh + 1) % 4 * 8 + yc))
-
-    def forward(k):
-        @pl.when(k < 3)
-        def _():
-            down(k).start()
-
-        @pl.when(k >= 5)
-        def _():
-            up(k).start()
-
-    for i in range(1, 8):
-        out_copy(i).start()
-    forward(yc)
-    unpack(3 + yc, rec, pot, levels[0])
+        return remote(rec.at[3 + k], rec.at[k - 5], fsem.at[k], rsem.at[k - 5], (b, above + yc))
+
+    def along_x(i, src, dst, sem):
+        return remote(src, dst, psem.at[sem], psem.at[sem + 1], ((x + i) % 4 * 2 + lower, d))
 
     @pl.loop(1, 8)
     def _(i):
-        k = (yc + 8 - i) % 8
-        in_copy(k).wait_recv()
-        forward(k)
-        unpack(3 + k, rec, pot, levels[0])
+        k = (yc + i) % 8
+        for j in range(4):
+            for o in range(2):
+                send[k, o, j] = orb[2 * k + o, j].astype(bf16)
+        out_copy(k).start()
+
+    for j in range(4):
+        for o in range(2):
+            rec[3 + yc, o, j] = orb[2 * yc + o, j].astype(bf16)
+
+    wait_bytes(potp.at[0:7], psem.at[1])
+    for i in range(1, 4):
+        along_x(i, potp, potg.at[x], 4).start()
+    potg[x] = potp[...]
+    wait_bytes(poth, psem.at[3])
+    for i in range(1, 4):
+        along_x(i, poth, poti.at[x], 6).start()
+    poti[x] = poth[...]
+
+    for k in (0, 7, 1, 6, 2, 5, 3, 4):
+
+        @pl.when(yc != k)
+        def _():
+            in_copy(k).wait_recv()
+
+        if k < 3:
+            down(k).start()
+        if k >= 5:
+            up(k).start()
+        unpack(3 + k, rec, levels[0])
+
+    wait_bytes(potg.at[0:3], psem.at[5])
+
+    @pl.loop(0, 8)
+    def _(s):
+        for i in range(4):
+            pot[12 + 4 * s + i] = scaled(potg[i, s])
 
     step = functools.partial(advance, levels=levels, pot=pot, circulant=circulant, sendf=sendf)
     for k in range(1, 7):
@@ -189,33 +231,52 @@
 
         @pl.loop(0, 2)
         def _(t):
-            step(k, 12 + 2 * k + planes * t, planes)
-
+            step(k, [(12 + 2 * k + planes * t, planes)])
+
+    own = pl.ds(b * 16 + yc * 2, 2)
+
+    def deliver(to):
+        @pl.loop(0, 8)
+        def _(i):
+            band = (b + i) % 8
+            q = to * 8 + band
+
+            @pl.when(q != me)
+            def _():
+                remote(sendf.at[q], gath.at[own], gsem.at[0], gsem.at[1], (band, zh * 8 + to)).start()
+
+    deliver(3)
+    deliver(4)
+
+    wait_bytes(poti.at[0:3], psem.at[7])
     for s in range(3):
-        up(5 + s).wait_recv()
-        down(s).wait_recv()
+        for i in range(4):
+            pot[4 * s + i] = scaled(poti[i, s])
+            pot[44 + 4 * s + i] = scaled(poti[i, 3 + s])
 
     @pl.loop(0, 3)
     def _(s):
-        unpack(s, rec, pot, levels[0])
-        unpack(11 + s, rec, pot, levels[0])
-
-    for k in range(1, 7):
-
-        @pl.loop(0, 2)
-        def _(t):
-            step(k, 2 * k + t * (44 - 4 * k), 12)
-
-    own = pl.ds(b * 16 + yc * 2, 2)
+        up(7 - s).wait_recv()
+        down(s).wait_recv()
+        unpack(2 - s, rec, levels[0])
+        unpack(11 + s, rec, levels[0])
+        for k in range(1, 7):
+            step(k, [(8 - 4 * s + 2 * k, 4), (44 + 4 * s - 2 * k, 4)])
+        deliver(2 - s)
+        deliver(5 + s)
+
     gath[own] = sendf[me]
 
-    @pl.loop(1, 64)
-    def _(i):
-        q = (me + i) % 64
-        remote(sendf.at[q], gath.at[own], gsem.at[0], gsem.at[1], (q % 8, zh * 8 + q // 8)).start()
-
-    for i in range(1, 8):
-        out_copy(i).wait_send()
+    wait_bytes(potp.at[0:7], psem.at[0])
+
+    @pl.when((yc < 3) | (yc >= 5))
+    def _():
+        wait_bytes(potp, psem.at[2])
+
+    wait_bytes(potg.at[0:3], psem.at[4])
+    wait_bytes(poti.at[0:3], psem.at[6])
+    for i in range(1, 8):
+        out_copy((yc + i) % 8).wait_send()
     for k in (0, 1, 2):
         down(k).wait_send()
     for k in (5, 6, 7):
@@ -301,8 +362,13 @@
         scratch_shapes=[
             pltpu.VMEM((16, 4, 32, 128), f32),
             pltpu.VMEM((4, 32, 128), f32),
-            pltpu.VMEM((8, 3, 4, 32, 128), bf16),
-            pltpu.VMEM((14, 3, 4, 32, 128), bf16),
+            pltpu.VMEM((4, 32, 128), bf16),
+            pltpu.VMEM((8, 32, 128), bf16),
+            pltpu.VMEM((6, 32, 128), bf16),
+            pltpu.VMEM((4, 8, 32, 128), bf16),
+            pltpu.VMEM((4, 6, 32, 128), bf16),
+            pltpu.VMEM((8, 2, 4, 32, 128), bf16),
+            pltpu.VMEM((14, 2, 4, 32, 128), bf16),
             pltpu.VMEM((56, 32, 128), f32),
             pltpu.VMEM((256, 128), bf16),
             pltpu.VMEM((64, 2, 16, 128), bf16),
@@ -321,7 +387,7 @@
             pltpu.VMEM((8, 16, 16, 128), f32),
         ]
         + [pltpu.VMEM((56, 2, 48, 128), f32)] * 6
-        + [dma((2,)), dma((8,)), dma((14,)), dma((8,)), dma((2,)), dma((8,)), dma((8,)), dma((8,)), dma((8,))],
+        + [dma((2,)), dma((8,)), dma((8,)), dma((14,)), dma((8,)), dma((2,)), dma((8,)), dma((8,)), dma((8,)), dma((8,))],
         compiler_params=pltpu.CompilerParams(collective_id=0, has_side_effects=True, vmem_limit_bytes=60 << 20),
     )(orbitals, potential)
 

time: 79.3 us -> 73.8 us (0.931)
  Pallas kernels: 76.9 us -> 71.4 us
    pallas_call x1, Pallas kernels: 76.9 us -> 71.4 us  [body(): pl.pallas_call(kernel, out_shape=jax.ShapeDtypeStruct((16, 4, 32, 128), f...]
where the time goes in v3:
time: 73.8 us; the launch traced here: 73.7 us
  Pallas kernels  71.4 us (97%)
  local copies, waits for them, and re-layouts  2.29 us (3%)
    pallas_call x1, Pallas kernels, body(): pl.pallas_call(kernel, out_shape=jax.ShapeDtypeStruct((16, 4, 32, 128), f...  71.4 us
    unnamed x1, local copies, waits for them, and re-layouts  2.29 us

profile of v3, /device:TPU:1, one launch (start us, length us, event | category | flops | bytes accessed | tf_op | source)
XLA Modules:
  0.0 73.7 jit_solution(1282592920218854716)
XLA Ops:
  0.0 71.4 %shard_map.28 = f32[16,4,32,128]{3,2,1,0:T(8,128)} custom-call(f32[16,4,32,128]{3,2,1,0:T(8,128)} %orb_hbm.1, f32[4,32,128]{2,1,0:T(8,128)} %pot_hbm.1), custom_call_target="tpu_custom_call" | custom-call | tf_op jit(solution)/shard_map/pallas_call | solution.py:357
  71.4 2.3 %copy.4 = f32[16,4,32,128]{3,2,1,0:T(8,128)} copy(f32[16,4,32,128]{3,2,1,0:T(8,128)} %shard_map.28) | data formatting | bytes 2097152

commit v4 on v3

v4 whole, which is shorter than its diff:
```python
import functools

import jax
import jax.numpy as jnp
from jax import lax
from jax.experimental import pallas as pl
from jax.experimental.pallas import tpu as pltpu
from jax.sharding import PartitionSpec as P

MESH = pl.DeviceIdType.MESH
f32, bf16 = jnp.float32, jnp.bfloat16

centre = 5.5
half = 4.5
SCALE = 2.0 / half
DIAGONAL = 0.5 * 7.5 - centre
FIRST = -0.5 * (4.0 / 3.0) * SCALE
SECOND = -1.0 / 16.0

VMEM = pl.BlockSpec(memory_space=pltpu.VMEM)
ANY = pl.BlockSpec(memory_space=pl.ANY)


def remote(src, dst, send_sem, recv_sem, device):
    return pltpu.make_async_remote_copy(
        src_ref=src, dst_ref=dst, send_sem=send_sem, recv_sem=recv_sem, device_id=device, device_id_type=MESH
    )


def wait_bytes(ref, sem):
    pltpu.make_async_copy(ref, ref, sem).wait()


def put(dst, p, o, v):
    dst[p, o, 8:40] = v
    dst[p, o, 0:8] = v[24:32]
    dst[p, o, 40:48] = v[0:8]


def unpack(slot, o, rec, field):
    for i in range(4):
        put(field, 4 * slot + i, o, rec[o, slot, i].astype(f32))


def scaled(plane):
    return (plane.astype(f32) + DIAGONAL) * SCALE


def advance(k, o, segments, levels, pot, circulant, sendf):
    src, prev = levels[k - 1], levels[k - 2]
    for first, planes in segments:
        window = [src[first - 2 + j, o, 8:40] for j in range(planes + 4)]
        v = jnp.concatenate(window[2:-2], axis=0)
        high = v.astype(bf16)
        low = (v - high.astype(f32)).astype(bf16)
        z = jnp.dot(jnp.concatenate([high, low], axis=1), circulant[...], preferred_element_type=f32)
        for i in range(planes):
            p = first + i
            s1 = window[i + 1] + window[i + 3]
            s2 = window[i] + window[i + 4]
            s1 = s1 + (src[p, o, 7:39] + src[p, o, 9:41])
            s2 = s2 + (src[p, o, 6:38] + src[p, o, 10:42])
            w = pot[p] * window[i + 2] + (s1 + z[32 * i : 32 * i + 32] + s2 * SECOND) * FIRST
            w = w * 0.5 if k == 1 else w - prev[p, o, 8:40]
            if k < 6:
                put(levels[k], p, o, w)
            else:
                w = w.astype(bf16)
                sendf[2 * (p - 12), o] = w[0:16]
                sendf[2 * (p - 12) + 1, o] = w[16:32]


def inverse_factor(m):
    n, nb = 128, 16
    row = lax.broadcasted_iota(jnp.int32, (nb, n), 0)
    lane = lax.broadcasted_iota(jnp.int32, (nb, n), 1)
    out = []
    for k in range(n // nb):
        at, lo = k * nb, (k + 1) * nb
        x = m[at:lo]
        cols = [jnp.broadcast_to(x[:, at + t : at + t + 1], (nb, n)) for t in range(nb)]
        own = (lane >= at) & (lane < lo)
        x = jnp.where(own, jnp.where(lane - at == row, 1.0, 0.0), x)
        w = jnp.zeros_like(x)
        for t in range(nb):
            here = row == t
            pivot = jnp.broadcast_to(cols[t][t : t + 1], (nb, n))
            inv = 1.0 / pivot
            r = jnp.broadcast_to(x[t : t + 1], (nb, n))
            w = jnp.where(here, r * lax.rsqrt(pivot), w)
            mult = jnp.where(here, 1.0 - inv, cols[t] * inv)
            x = x - mult * r
            for u in range(t + 1, nb):
                cols[u] = cols[u] - mult * jnp.broadcast_to(cols[u][t : t + 1], (nb, n))
        out.append(jnp.where(lane < lo, w, 0.0))
        if lo < n:
            below = m[lo:]
            lane_b = lax.broadcasted_iota(jnp.int32, below.shape, 1)
            padded = [jnp.zeros((at, n), f32)] * (at > 0) + [x, jnp.zeros((n - lo, n), f32)]
            change = jnp.dot(
                below, jnp.concatenate(padded, 0), precision=lax.Precision.HIGHEST, preferred_element_type=f32
            )
            kept = jnp.where((lane_b >= at) & (lane_b < lo), 0.0, below)
            m = jnp.concatenate([m[:lo], kept - change], axis=0)
    return out


def kernel(
    orb_hbm, pot_hbm, out_hbm,
    orb, potv, potb, potp, poth, potg, poti, send, rec, pot, circulant, sendf, gath,
    part, r1, q1, r2, q2, gram_ref, t_ref, rot, sendr, *rest
):
    levels, (lsem, psem, ssem, rsem, fsem, gsem, asem, bsem, csem, osem) = rest[:6], rest[6:]
    b, d = lax.axis_index("band"), lax.axis_index("dom")
    yc, zh = d % 8, d // 8
    x, lower = b // 2, b % 2
    me = yc * 8 + b
    above, below = (zh + 1) % 4 * 8, (zh + 3) % 4 * 8

    loadp = pltpu.make_async_copy(pot_hbm, potv, lsem.at[1])
    loadp.start()
    load = pltpu.make_async_copy(orb_hbm, orb, lsem.at[0])
    load.start()

    barrier = pltpu.get_barrier_semaphore()

    def greet(device):
        pl.semaphore_signal(barrier, inc=1, device_id=device, device_id_type=MESH)

    @pl.loop(1, 64)
    def _(i):
        q = (me + i) % 64
        greet((q % 8, zh * 8 + q // 8))

    @pl.loop(0, 8)
    def _(k):
        greet((b, above + k))
        greet((b, below + k))

    greet((b, (zh + 2) % 4 * 8 + yc))
    for i in range(1, 4):
        greet((x * 2 + 1 - lower, (zh + i) % 4 * 8 + yc))

    r = lax.broadcasted_iota(jnp.int32, (128, 128), 0)
    c = lax.broadcasted_iota(jnp.int32, (128, 128), 1)
    apart = (r - c + 128) % 128
    near = jnp.where((apart == 1) | (apart == 127), 1.0, 0.0)
    far = jnp.where((apart == 2) | (apart == 126), SECOND, 0.0)
    for h in range(2):
        circulant[h * 128 : (h + 1) * 128] = (near + far).astype(bf16)

    loadp.wait()
    potb[...] = potv[...].astype(bf16)
    potp[yc] = potb[x]
    pl.semaphore_wait(barrier, 83)

    for i in range(1, 8):
        remote(potb.at[x], potp.at[yc], psem.at[0], psem.at[1], (b, zh * 8 + (yc + i) % 8)).start()

    @pl.when(yc < 3)
    def _():
        for k in range(8):
            remote(potb.at[x], poth.at[3 + yc], psem.at[2], psem.at[3], (b, below + k)).start()

    @pl.when(yc >= 5)
    def _():
        for k in range(8):
            remote(potb.at[x], poth.at[yc - 5], psem.at[2], psem.at[3], (b, above + k)).start()

    load.wait()

    def out_copy(k, o):
        return remote(send.at[o, k], rec.at[o, 3 + yc], ssem.at[o, k], rsem.at[o, 3 + yc], (b, zh * 8 + k))

    def in_copy(k, o):
        return remote(send.at[o, k], rec.at[o, 3 + k], ssem.at[o, 0], rsem.at[o, 3 + k], (b, zh * 8 + k))

    def down(k, o):
        return remote(rec.at[o, 3 + k], rec.at[o, 11 + k], fsem.at[o, k], rsem.at[o, 11 + k], (b, below + yc))

    def up(k, o):
        return remote(rec.at[o, 3 + k], rec.at[o, k - 5], fsem.at[o, k], rsem.at[o, k - 5], (b, above + yc))

    def along_x(i, src, dst, sem):
        return remote(src, dst, psem.at[sem], psem.at[sem + 1], ((x + i) % 4 * 2 + lower, d))

    for o in range(2):

        @pl.loop(1, 8)
        def _(i):
            k = (yc + i) % 8
            for j in range(4):
                send[o, k, j] = orb[2 * k + o, j].astype(bf16)
            out_copy(k, o).start()

        for j in range(4):
            rec[o, 3 + yc, j] = orb[2 * yc + o, j].astype(bf16)

        if o == 0:
            for i in range(1, 8):
                wait_bytes(send.at[0, 0], ssem.at[0, (yc + i) % 8])

    wait_bytes(potp.at[0:7], psem.at[1])
    for i in range(1, 4):
        along_x(i, potp, potg.at[x], 4).start()
    potg[x] = potp[...]
    wait_bytes(poth, psem.at[3])
    for i in range(1, 4):
        along_x(i, poth, poti.at[x], 6).start()
    poti[x] = poth[...]

    def receive(o):
        for k in (0, 7, 1, 6, 2, 5, 3, 4):

            @pl.when(yc != k)
            def _():
                in_copy(k, o).wait_recv()

            if k < 3:
                down(k, o).start()
            if k >= 5:
                up(k, o).start()
            unpack(3 + k, o, rec, levels[0])

    step = functools.partial(advance, levels=levels, pot=pot, circulant=circulant, sendf=sendf)
    receive(0)
    receive(1)
    wait_bytes(potg.at[0:3], psem.at[5])

    @pl.loop(0, 8)
    def _(s):
        for i in range(4):
            pot[12 + 4 * s + i] = scaled(potg[i, s])

    @pl.loop(0, 2)
    def _(o):
        for k in range(1, 7):
            step(k, o, [(12 + 2 * k, 32 - 4 * k)])

    own = pl.ds(b * 16 + yc * 2, 2)

    def deliver(to):
        @pl.loop(0, 8)
        def _(i):
            band = (b + i) % 8
            q = to * 8 + band

            @pl.when(q != me)
            def _():
                remote(sendf.at[q], gath.at[own], gsem.at[0], gsem.at[1], (band, zh * 8 + to)).start()

    deliver(3)
    deliver(4)

    wait_bytes(poti.at[0:3], psem.at[7])
    for s in range(3):
        for i in range(4):
            pot[4 * s + i] = scaled(poti[i, s])
            pot[44 + 4 * s + i] = scaled(poti[i, 3 + s])

    def halo(s, o):
        up(7 - s, o).wait_recv()
        down(s, o).wait_recv()
        unpack(2 - s, o, rec, levels[0])
        unpack(11 + s, o, rec, levels[0])

    for s in range(3):
        halo(s, 0)
    for k in range(1, 7):
        step(k, 0, [(2 * k, 12), (44 - 2 * k, 12)])

    @pl.loop(0, 3)
    def _(s):
        halo(s, 1)
        for k in range(1, 7):
            step(k, 1, [(8 - 4 * s + 2 * k, 4), (44 + 4 * s - 2 * k, 4)])
        deliver(2 - s)
        deliver(5 + s)

    gath[own] = sendf[me]

    wait_bytes(potp.at[0:7], psem.at[0])

    @pl.when((yc < 3) | (yc >= 5))
    def _():
        wait_bytes(potp, psem.at[2])

    wait_bytes(potg.at[0:3], psem.at[4])
    wait_bytes(poti.at[0:3], psem.at[6])
    for o in range(2):
        for i in range(1, 8):
            if o == 1:
                out_copy((yc + i) % 8, o).wait_send()
        for k in (0, 1, 2):
            down(k, o).wait_send()
        for k in (5, 6, 7):
            up(k, o).wait_send()
    wait_bytes(gath.at[0:126], gsem.at[1])

    t = jnp.swapaxes(gath[...].astype(f32), 0, 1).astype(bf16)
    t_ref[...] = t
    cells = jnp.concatenate([t[j] for j in range(16)], axis=1)
    gram = lax.dot_general(cells, cells, (((1,), (1,)), ((), ())), preferred_element_type=f32)
    part[...] = gram.reshape(32, 4, 128)
    mine, level = x * 8 + yc, zh * 2 + lower

    def among(i):
        j = (mine + i) % 32
        return j, (j // 8 * 2 + lower, zh * 8 + j % 8)

    @pl.loop(1, 32)
    def _(i):
        j, device = among(i)
        remote(part.at[j], r1.at[mine], asem.at[0], asem.at[1], device).start()

    r1[mine] = part[mine]
    wait_bytes(r1.at[0:31], asem.at[1])
    q1[...] = jnp.sum(r1[...], axis=0)
    for i in range(1, 8):
        j = (level + i) % 8
        remote(q1, r2.at[level], asem.at[2], asem.at[3], (x * 2 + j % 2, j // 2 * 8 + yc)).start()
    r2[level] = q1[...]
    wait_bytes(r2.at[0:7], asem.at[3])
    q2[...] = jnp.sum(r2[...], axis=0)

    @pl.loop(1, 32)
    def _(i):
        j, device = among(i)
        remote(q2, gram_ref.at[mine], asem.at[4], asem.at[5], device).start()

    gram_ref[mine] = q2[...]
    wait_bytes(gram_ref.at[0:31], asem.at[5])
    inverse = inverse_factor(gram_ref[...].reshape(128, 128) * (1.0 / 2.0**19))
    w = jnp.concatenate([block.astype(bf16) for block in inverse], axis=0)
    for j in range(16):
        rot[j] = jnp.dot(w, t_ref[j], preferred_element_type=f32)

    def turned(k):
        return jnp.swapaxes(rot[:, pl.ds(pl.multiple_of(16 * k, 16), 16), :], 0, 1).astype(bf16)

    def cells_of(band):
        return out_hbm.at[:, band // 2, pl.ds(pl.multiple_of(band % 2 * 16, 16), 16), :]

    def back_copy(i):
        k = (b + i) % 8
        return remote(sendr.at[k], cells_of(b), bsem.at[i], csem.at[b], (k, d))

    @pl.loop(1, 8)
    def _(i):
        k = (b + i) % 8
        sendr[k] = turned(k)
        back_copy(i).start()

    sendr[b] = turned(b)
    stay = pltpu.make_async_copy(sendr.at[b], cells_of(b), osem.at[0])
    stay.start()

    wait_bytes(gath.at[0:126], gsem.at[0])
    wait_bytes(r1.at[0:31], asem.at[0])
    wait_bytes(r2.at[0:7], asem.at[2])
    wait_bytes(r1.at[0:31], asem.at[4])
    for i in range(1, 8):
        back_copy(i).wait_send()
    for i in range(1, 8):
        k = (b + 8 - i) % 8
        remote(sendr.at[k], cells_of(k), bsem.at[0], csem.at[k], (k, d)).wait_recv()
    stay.wait()


def body(orbitals, potential):
    dma = pltpu.SemaphoreType.DMA
    rotated = pl.pallas_call(
        kernel,
        out_shape=jax.ShapeDtypeStruct((16, 4, 32, 128), bf16),
        in_specs=[ANY, ANY],
        out_specs=ANY,
        scratch_shapes=[
            pltpu.VMEM((16, 4, 32, 128), f32),
            pltpu.VMEM((4, 32, 128), f32),
            pltpu.VMEM((4, 32, 128), bf16),
            pltpu.VMEM((8, 32, 128), bf16),
            pltpu.VMEM((6, 32, 128), bf16),
            pltpu.VMEM((4, 8, 32, 128), bf16),
            pltpu.VMEM((4, 6, 32, 128), bf16),
            pltpu.VMEM((2, 8, 4, 32, 128), bf16),
            pltpu.VMEM((2, 14, 4, 32, 128), bf16),
            pltpu.VMEM((56, 32, 128), f32),
            pltpu.VMEM((256, 128), bf16),
            pltpu.VMEM((64, 2, 16, 128), bf16),
            pltpu.VMEM((128, 16, 128), bf16),
            pltpu.VMEM((32, 4, 128), f32),
            pltpu.VMEM((32, 4, 128), f32),
            pltpu.VMEM((4, 128), f32),
            pltpu.VMEM((8, 4, 128), f32),
            pltpu.VMEM((4, 128), f32),
            pltpu.VMEM((32, 4, 128), f32),
            pltpu.VMEM((16, 128, 128), bf16),
            pltpu.VMEM((16, 128, 128), f32),
            pltpu.VMEM((8, 16, 16, 128), bf16),
        ]
        + [pltpu.VMEM((56, 2, 48, 128), f32)] * 6
        + [dma((2,)), dma((8,)), dma((2, 8)), dma((2, 14)), dma((2, 8)), dma((2,)), dma((8,)), dma((8,)), dma((8,)), dma((8,))],
        compiler_params=pltpu.CompilerParams(collective_id=0, has_side_effects=True, vmem_limit_bytes=60 << 20),
    )(orbitals, potential)
    return rotated.astype(f32)


def solution(mesh):
    placed = (P("band", "dom", None, None), P("dom", None, None))
    return jax.shard_map(
        body, mesh=mesh, in_specs=placed, out_specs=P("band", "dom", None, None), check_vma=False
    )
```

time: 73.8 us -> 69.8 us (0.946)
  Pallas kernels: 71.4 us -> 67.6 us
  local copies, waits for them, and re-layouts: 2.29 us -> 0 us
  other arithmetic: 0 us -> 2.14 us
    pallas_call x1, Pallas kernels: 71.4 us -> 67.6 us  [body(): pl.pallas_call(kernel, out_shape=jax.ShapeDtypeStruct((16, 4, 32, 128), b...]
    unnamed x1 -> x0, local copies, waits for them, and re-layouts: 2.29 us -> none
    convert_element_type x0 -> x1, other arithmetic: none -> 2.14 us  [body(): return rotated.astype(f32)]
where the time goes in v4:
time: 69.8 us; the launch traced here: 69.7 us
  Pallas kernels  67.6 us (97%)
  other arithmetic  2.14 us (3%)
    pallas_call x1, Pallas kernels, body(): pl.pallas_call(kernel, out_shape=jax.ShapeDtypeStruct((16, 4, 32, 128), b...  67.6 us
    convert_element_type x1, other arithmetic, body(): return rotated.astype(f32)  2.14 us

profile of v4, /device:TPU:1, one launch (start us, length us, event | category | flops | bytes accessed | tf_op | source)
XLA Modules:
  0.0 69.7 jit_solution(16158266331463937305)
XLA Ops:
  0.0 67.6 %shard_map.28 = bf16[16,4,32,128]{3,2,1,0:T(8,128)(2,1)} custom-call(f32[16,4,32,128]{3,2,1,0:T(8,128)} %orb_hbm.1, f32[4,32,128]{2,1,0:T(8,128)} %pot_hbm.1), custom_call_target="tpu_custom_call" | custom-call | tf_op jit(solution)/shard_map/pallas_call | solution.py:372
  67.6 2.1 %convert_element_type.3 = f32[16,4,32,128]{3,2,1,0:T(8,128)} convert(bf16[16,4,32,128]{3,2,1,0:T(8,128)(2,1)} %shard_map.28) | non-fusion elementwise | flops 262144 | bytes 1572864 | tf_op jit(solution)/shard_map/convert_element_type | solution.py:405

commit v5 on v4

--- a/solution.py
+++ b/solution.py
@@ -110,7 +110,7 @@
     orb, potv, potb, potp, poth, potg, poti, send, rec, pot, circulant, sendf, gath,
     part, r1, q1, r2, q2, gram_ref, t_ref, rot, sendr, *rest
 ):
-    levels, (lsem, psem, ssem, rsem, fsem, gsem, asem, bsem, csem, osem) = rest[:6], rest[6:]
+    levels, (lsem, psem, ssem, rsem, fsem, dsem, gsem, asem, bsem, csem, osem) = rest[:6], rest[6:]
     b, d = lax.axis_index("band"), lax.axis_index("dom")
     yc, zh = d % 8, d // 8
     x, lower = b // 2, b % 2
@@ -127,15 +127,17 @@
     def greet(device):
         pl.semaphore_signal(barrier, inc=1, device_id=device, device_id_type=MESH)
 
-    @pl.loop(1, 64)
-    def _(i):
-        q = (me + i) % 64
-        greet((q % 8, zh * 8 + q // 8))
+    for i in range(1, 8):
+        greet((b, zh * 8 + (yc + i) % 8))
 
     @pl.loop(0, 8)
     def _(k):
         greet((b, above + k))
         greet((b, below + k))
+
+    @pl.loop(8, 64)
+    def _(i):
+        greet(((b + i // 8) % 8, zh * 8 + i % 8))
 
     greet((b, (zh + 2) % 4 * 8 + yc))
     for i in range(1, 4):
@@ -181,20 +183,45 @@
     def up(k, o):
         return remote(rec.at[o, 3 + k], rec.at[o, k - 5], fsem.at[o, k], rsem.at[o, k - 5], (b, above + yc))
 
+    sibling = yc + 1 - 2 * (yc % 2)
+
+    def straight_down(k, o, i):
+        return remote(send.at[o, k], rec.at[o, 11 + yc], dsem.at[o, i], rsem.at[o, 11 + yc], (b, below + k))
+
+    def straight_up(k, o, i):
+        return remote(send.at[o, k], rec.at[o, yc - 5], dsem.at[o, i], rsem.at[o, yc - 5], (b, above + k))
+
     def along_x(i, src, dst, sem):
         return remote(src, dst, psem.at[sem], psem.at[sem + 1], ((x + i) % 4 * 2 + lower, d))
 
     for o in range(2):
+
+        for k in (yc, sibling):
+            for j in range(4):
+                send[o, k, j] = orb[2 * k + o, j].astype(bf16)
+
+        @pl.when(yc < 3)
+        def _():
+            straight_down(yc, o, 0).start()
+            straight_down(sibling, o, 1).start()
+
+        @pl.when(yc >= 5)
+        def _():
+            straight_up(yc, o, 0).start()
+            straight_up(sibling, o, 1).start()
 
         @pl.loop(1, 8)
         def _(i):
             k = (yc + i) % 8
-            for j in range(4):
-                send[o, k, j] = orb[2 * k + o, j].astype(bf16)
+
+            @pl.when(k != sibling)
+            def _():
+                for j in range(4):
+                    send[o, k, j] = orb[2 * k + o, j].astype(bf16)
+
             out_copy(k, o).start()
 
-        for j in range(4):
-            rec[o, 3 + yc, j] = orb[2 * yc + o, j].astype(bf16)
+        rec[o, 3 + yc] = send[o, yc]
 
         if o == 0:
             for i in range(1, 8):
@@ -209,22 +236,59 @@
         along_x(i, poth, poti.at[x], 6).start()
     poti[x] = poth[...]
 
-    def receive(o):
+    def forward(k, o):
+        @pl.when(yc // 2 != k // 2)
+        def _():
+            (down if k < 3 else up)(k, o).start()
+
+    def receive(o, to_forward):
         for k in (0, 7, 1, 6, 2, 5, 3, 4):
 
             @pl.when(yc != k)
             def _():
                 in_copy(k, o).wait_recv()
 
-            if k < 3:
-                down(k, o).start()
-            if k >= 5:
-                up(k, o).start()
+            if k in to_forward:
+                forward(k, o)
             unpack(3 + k, o, rec, levels[0])
 
     step = functools.partial(advance, levels=levels, pot=pot, circulant=circulant, sendf=sendf)
-    receive(0)
-    receive(1)
+
+    def inner(o):
+        for k in range(1, 7):
+            step(k, o, [(12 + 2 * k, 32 - 4 * k)])
+
+    own = b * 16 + yc * 2
+
+    def deliver(to, orbitals=(0, 1)):
+        @pl.loop(0, 8)
+        def _(i):
+            band = (b + 4 + i) % 8
+            q = to * 8 + band
+            part_of = pl.ds(orbitals[0], len(orbitals))
+
+            @pl.when(q != me)
+            def _():
+                remote(
+                    sendf.at[q, part_of],
+                    gath.at[pl.ds(own + orbitals[0], len(orbitals))],
+                    gsem.at[0],
+                    gsem.at[1],
+                    (band, zh * 8 + to),
+                ).start()
+
+    def halo(s, o):
+        up(7 - s, o).wait_recv()
+        down(s, o).wait_recv()
+        unpack(2 - s, o, rec, levels[0])
+        unpack(11 + s, o, rec, levels[0])
+
+    def piece(s):
+        for k in range(1, 7):
+            step(k, 1, [(8 - 4 * s + 2 * k, 4), (44 + 4 * s - 2 * k, 4)])
+
+    receive(0, (0, 7, 1, 6, 2, 5))
+    receive(1, (0, 7, 1, 6))
     wait_bytes(potg.at[0:3], psem.at[5])
 
     @pl.loop(0, 8)
@@ -232,23 +296,10 @@
         for i in range(4):
             pot[12 + 4 * s + i] = scaled(potg[i, s])
 
-    @pl.loop(0, 2)
-    def _(o):
-        for k in range(1, 7):
-            step(k, o, [(12 + 2 * k, 32 - 4 * k)])
-
-    own = pl.ds(b * 16 + yc * 2, 2)
-
-    def deliver(to):
-        @pl.loop(0, 8)
-        def _(i):
-            band = (b + i) % 8
-            q = to * 8 + band
-
-            @pl.when(q != me)
-            def _():
-                remote(sendf.at[q], gath.at[own], gsem.at[0], gsem.at[1], (band, zh * 8 + to)).start()
-
+    inner(0)
+    forward(2, 1)
+    forward(5, 1)
+    inner(1)
     deliver(3)
     deliver(4)
 
@@ -258,26 +309,26 @@
             pot[4 * s + i] = scaled(poti[i, s])
             pot[44 + 4 * s + i] = scaled(poti[i, 3 + s])
 
-    def halo(s, o):
-        up(7 - s, o).wait_recv()
-        down(s, o).wait_recv()
-        unpack(2 - s, o, rec, levels[0])
-        unpack(11 + s, o, rec, levels[0])
-
     for s in range(3):
         halo(s, 0)
     for k in range(1, 7):
         step(k, 0, [(2 * k, 12), (44 - 2 * k, 12)])
-
-    @pl.loop(0, 3)
+    deliver(0, (0,))
+    deliver(7, (0,))
+
+    @pl.loop(0, 2)
     def _(s):
         halo(s, 1)
-        for k in range(1, 7):
-            step(k, 1, [(8 - 4 * s + 2 * k, 4), (44 + 4 * s - 2 * k, 4)])
+        piece(s)
         deliver(2 - s)
         deliver(5 + s)
 
-    gath[own] = sendf[me]
+    halo(2, 1)
+    piece(2)
+    deliver(0, (1,))
+    deliver(7, (1,))
+
+    gath[pl.ds(own, 2)] = sendf[me]
 
     wait_bytes(potp.at[0:7], psem.at[0])
 
@@ -291,10 +342,17 @@
         for i in range(1, 8):
             if o == 1:
                 out_copy((yc + i) % 8, o).wait_send()
-        for k in (0, 1, 2):
-            down(k, o).wait_send()
-        for k in (5, 6, 7):
-            up(k, o).wait_send()
+        for k in (0, 1, 2, 5, 6, 7):
+
+            @pl.when(yc // 2 != k // 2)
+            def _():
+                wait_bytes(send.at[0, 0], fsem.at[o, k])
+
+        @pl.when((yc < 3) | (yc >= 5))
+        def _():
+            for i in range(2):
+                wait_bytes(send.at[0, 0], dsem.at[o, i])
+
     wait_bytes(gath.at[0:126], gsem.at[1])
 
     t = jnp.swapaxes(gath[...].astype(f32), 0, 1).astype(bf16)
@@ -304,28 +362,31 @@
     part[...] = gram.reshape(32, 4, 128)
     mine, level = x * 8 + yc, zh * 2 + lower
 
-    def among(i):
-        j = (mine + i) % 32
-        return j, (j // 8 * 2 + lower, zh * 8 + j % 8)
-
-    @pl.loop(1, 32)
-    def _(i):
-        j, device = among(i)
+    def others(send_to):
+        @pl.loop(0, 32)
+        def _(i):
+            col, row = (x + i // 8 + 2) % 4, (yc + i + 4) % 8
+
+            @pl.when(i != 20)
+            def _():
+                send_to(col * 8 + row, (col * 2 + lower, zh * 8 + row))
+
+    @others
+    def _(j, device):
         remote(part.at[j], r1.at[mine], asem.at[0], asem.at[1], device).start()
 
     r1[mine] = part[mine]
     wait_bytes(r1.at[0:31], asem.at[1])
     q1[...] = jnp.sum(r1[...], axis=0)
-    for i in range(1, 8):
+    for i in (4, 3, 5, 2, 6, 1, 7):
         j = (level + i) % 8
         remote(q1, r2.at[level], asem.at[2], asem.at[3], (x * 2 + j % 2, j // 2 * 8 + yc)).start()
     r2[level] = q1[...]
     wait_bytes(r2.at[0:7], asem.at[3])
     q2[...] = jnp.sum(r2[...], axis=0)
 
-    @pl.loop(1, 32)
-    def _(i):
-        j, device = among(i)
+    @others
+    def _(j, device):
         remote(q2, gram_ref.at[mine], asem.at[4], asem.at[5], device).start()
 
     gram_ref[mine] = q2[...]
@@ -399,7 +460,7 @@
             pltpu.VMEM((8, 16, 16, 128), bf16),
         ]
         + [pltpu.VMEM((56, 2, 48, 128), f32)] * 6
-        + [dma((2,)), dma((8,)), dma((2, 8)), dma((2, 14)), dma((2, 8)), dma((2,)), dma((8,)), dma((8,)), dma((8,)), dma((8,))],
+        + [dma((2,)), dma((8,)), dma((2, 8)), dma((2, 14)), dma((2, 8)), dma((2, 2)), dma((2,)), dma((8,)), dma((8,)), dma((8,)), dma((8,))],
         compiler_params=pltpu.CompilerParams(collective_id=0, has_side_effects=True, vmem_limit_bytes=60 << 20),
     )(orbitals, potential)
     return rotated.astype(f32)

time: 69.8 us -> 68.2 us (0.977)
  Pallas kernels: 67.6 us -> 65.9 us
    pallas_call x1, Pallas kernels: 67.6 us -> 65.9 us  [body(): pl.pallas_call(kernel, out_shape=jax.ShapeDtypeStruct((16, 4, 32, 128), b...]
where the time goes in v5:
time: 68.2 us; the launch traced here: 68.1 us
  Pallas kernels  65.9 us (97%)
  other arithmetic  2.14 us (3%)
    pallas_call x1, Pallas kernels, body(): pl.pallas_call(kernel, out_shape=jax.ShapeDtypeStruct((16, 4, 32, 128), b...  65.9 us
    convert_element_type x1, other arithmetic, body(): return rotated.astype(f32)  2.14 us

profile of v5, /device:TPU:1, one launch (start us, length us, event | category | flops | bytes accessed | tf_op | source)
XLA Modules:
  0.0 68.1 jit_solution(15733592437874312546)
XLA Ops:
  0.0 65.9 %shard_map.28 = bf16[16,4,32,128]{3,2,1,0:T(8,128)(2,1)} custom-call(f32[16,4,32,128]{3,2,1,0:T(8,128)} %orb_hbm.1, f32[4,32,128]{2,1,0:T(8,128)} %pot_hbm.1), custom_call_target="tpu_custom_call" | custom-call | tf_op jit(solution)/shard_map/pallas_call | solution.py:433
  66.0 2.1 %convert_element_type.3 = f32[16,4,32,128]{3,2,1,0:T(8,128)} convert(bf16[16,4,32,128]{3,2,1,0:T(8,128)(2,1)} %shard_map.28) | non-fusion elementwise | flops 262144 | bytes 1572864 | tf_op jit(solution)/shard_map/convert_element_type | solution.py:466

commit v6 on v5

--- a/solution.py
+++ b/solution.py
@@ -110,7 +110,7 @@
     orb, potv, potb, potp, poth, potg, poti, send, rec, pot, circulant, sendf, gath,
     part, r1, q1, r2, q2, gram_ref, t_ref, rot, sendr, *rest
 ):
-    levels, (lsem, psem, ssem, rsem, fsem, dsem, gsem, asem, bsem, csem, osem) = rest[:6], rest[6:]
+    levels, (lsem, psem, ssem, rsem, fsem, dsem, gsem, asem, bsem, csem, osem, ready) = rest[:6], rest[6:]
     b, d = lax.axis_index("band"), lax.axis_index("dom")
     yc, zh = d % 8, d // 8
     x, lower = b // 2, b % 2
@@ -135,10 +135,8 @@
         greet((b, above + k))
         greet((b, below + k))
 
-    @pl.loop(8, 64)
-    def _(i):
-        greet(((b + i // 8) % 8, zh * 8 + i % 8))
-
+    for i in range(1, 8):
+        greet(((b + i) % 8, d))
     greet((b, (zh + 2) % 4 * 8 + yc))
     for i in range(1, 4):
         greet((x * 2 + 1 - lower, (zh + i) % 4 * 8 + yc))
@@ -154,22 +152,29 @@
     loadp.wait()
     potb[...] = potv[...].astype(bf16)
     potp[yc] = potb[x]
-    pl.semaphore_wait(barrier, 83)
+    load.wait()
+
+    @pl.loop(0, 8)
+    def _(k):
+        for o in range(2):
+            for j in range(4):
+                send[o, k, j] = orb[2 * k + o, j].astype(bf16)
+
+    pl.semaphore_wait(barrier, 34)
 
     for i in range(1, 8):
         remote(potb.at[x], potp.at[yc], psem.at[0], psem.at[1], (b, zh * 8 + (yc + i) % 8)).start()
 
-    @pl.when(yc < 3)
-    def _():
-        for k in range(8):
-            remote(potb.at[x], poth.at[3 + yc], psem.at[2], psem.at[3], (b, below + k)).start()
-
-    @pl.when(yc >= 5)
-    def _():
-        for k in range(8):
-            remote(potb.at[x], poth.at[yc - 5], psem.at[2], psem.at[3], (b, above + k)).start()
-
-    load.wait()
+    def halo_planes():
+        @pl.when(yc < 3)
+        def _():
+            for k in range(8):
+                remote(potb.at[x], poth.at[3 + yc], psem.at[2], psem.at[3], (b, below + k)).start()
+
+        @pl.when(yc >= 5)
+        def _():
+            for k in range(8):
+                remote(potb.at[x], poth.at[yc - 5], psem.at[2], psem.at[3], (b, above + k)).start()
 
     def out_copy(k, o):
         return remote(send.at[o, k], rec.at[o, 3 + yc], ssem.at[o, k], rsem.at[o, 3 + yc], (b, zh * 8 + k))
@@ -196,10 +201,6 @@
 
     for o in range(2):
 
-        for k in (yc, sibling):
-            for j in range(4):
-                send[o, k, j] = orb[2 * k + o, j].astype(bf16)
-
         @pl.when(yc < 3)
         def _():
             straight_down(yc, o, 0).start()
@@ -210,20 +211,15 @@
             straight_up(yc, o, 0).start()
             straight_up(sibling, o, 1).start()
 
-        @pl.loop(1, 8)
-        def _(i):
-            k = (yc + i) % 8
-
-            @pl.when(k != sibling)
-            def _():
-                for j in range(4):
-                    send[o, k, j] = orb[2 * k + o, j].astype(bf16)
-
-            out_copy(k, o).start()
-
+        for i in (4, 3, 5, 2, 6, 1, 7):
+            out_copy((yc + i) % 8, o).start()
         rec[o, 3 + yc] = send[o, yc]
 
         if o == 0:
+            halo_planes()
+
+            for i in range(1, 8):
+                pl.semaphore_signal(ready, inc=1, device_id=((b + i) % 8, d), device_id_type=MESH)
             for i in range(1, 8):
                 wait_bytes(send.at[0, 0], ssem.at[0, (yc + i) % 8])
 
@@ -300,6 +296,7 @@
     forward(2, 1)
     forward(5, 1)
     inner(1)
+    pl.semaphore_wait(ready, 7)
     deliver(3)
     deliver(4)
 
@@ -460,7 +457,7 @@
             pltpu.VMEM((8, 16, 16, 128), bf16),
         ]
         + [pltpu.VMEM((56, 2, 48, 128), f32)] * 6
-        + [dma((2,)), dma((8,)), dma((2, 8)), dma((2, 14)), dma((2, 8)), dma((2, 2)), dma((2,)), dma((8,)), dma((8,)), dma((8,)), dma((8,))],
+        + [dma((2,)), dma((8,)), dma((2, 8)), dma((2, 14)), dma((2, 8)), dma((2, 2)), dma((2,)), dma((8,)), dma((8,)), dma((8,)), dma((8,)), pltpu.SemaphoreType.REGULAR],
         compiler_params=pltpu.CompilerParams(collective_id=0, has_side_effects=True, vmem_limit_bytes=60 << 20),
     )(orbitals, potential)
     return rotated.astype(f32)

time: 68.2 us -> 70.9 us (1.040)
  Pallas kernels: 65.9 us -> 68.6 us
    pallas_call x1, Pallas kernels: 65.9 us -> 68.6 us  [body(): pl.pallas_call(kernel, out_shape=jax.ShapeDtypeStruct((16, 4, 32, 128), b...]
where the time goes in v6:
time: 70.9 us; the launch traced here: 70.8 us
  Pallas kernels  68.6 us (97%)
  other arithmetic  2.14 us (3%)
    pallas_call x1, Pallas kernels, body(): pl.pallas_call(kernel, out_shape=jax.ShapeDtypeStruct((16, 4, 32, 128), b...  68.6 us
    convert_element_type x1, other arithmetic, body(): return rotated.astype(f32)  2.14 us

profile of v6, /device:TPU:1, one launch (start us, length us, event | category | flops | bytes accessed | tf_op | source)
XLA Modules:
  0.0 70.8 jit_solution(18130361764338014075)
XLA Ops:
  0.0 68.6 %shard_map.28 = bf16[16,4,32,128]{3,2,1,0:T(8,128)(2,1)} custom-call(f32[16,4,32,128]{3,2,1,0:T(8,128)} %orb_hbm.1, f32[4,32,128]{2,1,0:T(8,128)} %pot_hbm.1), custom_call_target="tpu_custom_call" | custom-call | tf_op jit(solution)/shard_map/pallas_call | solution.py:430
  68.6 2.1 %convert_element_type.3 = f32[16,4,32,128]{3,2,1,0:T(8,128)} convert(bf16[16,4,32,128]{3,2,1,0:T(8,128)(2,1)} %shard_map.28) | non-fusion elementwise | flops 262144 | bytes 1572864 | tf_op jit(solution)/shard_map/convert_element_type | solution.py:463

commit v7 on v5

--- a/solution.py
+++ b/solution.py
@@ -110,7 +110,7 @@
     orb, potv, potb, potp, poth, potg, poti, send, rec, pot, circulant, sendf, gath,
     part, r1, q1, r2, q2, gram_ref, t_ref, rot, sendr, *rest
 ):
-    levels, (lsem, psem, ssem, rsem, fsem, dsem, gsem, asem, bsem, csem, osem) = rest[:6], rest[6:]
+    levels, (lsem, psem, ssem, rsem, fsem, dsem, gsem, asem, bsem, csem, osem, ready) = rest[:6], rest[6:]
     b, d = lax.axis_index("band"), lax.axis_index("dom")
     yc, zh = d % 8, d // 8
     x, lower = b // 2, b % 2
@@ -135,10 +135,8 @@
         greet((b, above + k))
         greet((b, below + k))
 
-    @pl.loop(8, 64)
-    def _(i):
-        greet(((b + i // 8) % 8, zh * 8 + i % 8))
-
+    for i in range(1, 8):
+        greet(((b + i) % 8, d))
     greet((b, (zh + 2) % 4 * 8 + yc))
     for i in range(1, 4):
         greet((x * 2 + 1 - lower, (zh + i) % 4 * 8 + yc))
@@ -154,10 +152,7 @@
     loadp.wait()
     potb[...] = potv[...].astype(bf16)
     potp[yc] = potb[x]
-    pl.semaphore_wait(barrier, 83)
-
-    for i in range(1, 8):
-        remote(potb.at[x], potp.at[yc], psem.at[0], psem.at[1], (b, zh * 8 + (yc + i) % 8)).start()
+    pl.semaphore_wait(barrier, 34)
 
     @pl.when(yc < 3)
     def _():
@@ -169,6 +164,9 @@
         for k in range(8):
             remote(potb.at[x], poth.at[yc - 5], psem.at[2], psem.at[3], (b, above + k)).start()
 
+    for i in range(1, 8):
+        remote(potb.at[x], potp.at[yc], psem.at[0], psem.at[1], (b, zh * 8 + (yc + i) % 8)).start()
+
     load.wait()
 
     def out_copy(k, o):
@@ -224,6 +222,8 @@
         rec[o, 3 + yc] = send[o, yc]
 
         if o == 0:
+            for i in range(1, 8):
+                pl.semaphore_signal(ready, inc=1, device_id=((b + i) % 8, d), device_id_type=MESH)
             for i in range(1, 8):
                 wait_bytes(send.at[0, 0], ssem.at[0, (yc + i) % 8])
 
@@ -300,6 +300,7 @@
     forward(2, 1)
     forward(5, 1)
     inner(1)
+    pl.semaphore_wait(ready, 7)
     deliver(3)
     deliver(4)
 
@@ -316,10 +317,11 @@
     deliver(0, (0,))
     deliver(7, (0,))
 
-    @pl.loop(0, 2)
-    def _(s):
+    for s in range(2):
         halo(s, 1)
-        piece(s)
+    for k in range(1, 7):
+        step(k, 1, [(4 + 2 * k, 8), (44 - 2 * k, 8)])
+    for s in range(2):
         deliver(2 - s)
         deliver(5 + s)
 
@@ -363,12 +365,9 @@
     mine, level = x * 8 + yc, zh * 2 + lower
 
     def others(send_to):
-        @pl.loop(0, 32)
-        def _(i):
-            col, row = (x + i // 8 + 2) % 4, (yc + i + 4) % 8
-
-            @pl.when(i != 20)
-            def _():
+        for i in range(32):
+            if i != 20:
+                col, row = (x + (i // 8 + 2) % 4) % 4, (yc + (i + 4) % 8) % 8
                 send_to(col * 8 + row, (col * 2 + lower, zh * 8 + row))
 
     @others
@@ -434,7 +433,7 @@
         kernel,
         out_shape=jax.ShapeDtypeStruct((16, 4, 32, 128), bf16),
         in_specs=[ANY, ANY],
-        out_specs=ANY,
+        out_specs=VMEM,
         scratch_shapes=[
             pltpu.VMEM((16, 4, 32, 128), f32),
             pltpu.VMEM((4, 32, 128), f32),
@@ -460,8 +459,8 @@
             pltpu.VMEM((8, 16, 16, 128), bf16),
         ]
         + [pltpu.VMEM((56, 2, 48, 128), f32)] * 6
-        + [dma((2,)), dma((8,)), dma((2, 8)), dma((2, 14)), dma((2, 8)), dma((2, 2)), dma((2,)), dma((8,)), dma((8,)), dma((8,)), dma((8,))],
-        compiler_params=pltpu.CompilerParams(collective_id=0, has_side_effects=True, vmem_limit_bytes=60 << 20),
+        + [dma((2,)), dma((8,)), dma((2, 8)), dma((2, 14)), dma((2, 8)), dma((2, 2)), dma((2,)), dma((8,)), dma((8,)), dma((8,)), dma((8,)), pltpu.SemaphoreType.REGULAR],
+        compiler_params=pltpu.CompilerParams(collective_id=0, has_side_effects=True, vmem_limit_bytes=54400 << 10),
     )(orbitals, potential)
     return rotated.astype(f32)
 

time: 68.2 us -> 66.3 us (0.972)
  Pallas kernels: 65.9 us -> 64.2 us
  other arithmetic: 2.14 us -> 1.1 us
  local copies, waits for them, and re-layouts: 0 us -> 0.84 us
    pallas_call x1, Pallas kernels: 65.9 us -> 64.2 us  [body(): pl.pallas_call(kernel, out_shape=jax.ShapeDtypeStruct((16, 4, 32, 128), b...]
    convert_element_type x1, other arithmetic: 2.14 us -> 1.1 us  [body(): return rotated.astype(f32)]
    unnamed x0 -> x2, local copies, waits for them, and re-layouts: none -> 0.84 us
where the time goes in v7:
time: 66.3 us; the launch traced here: 66.2 us
  Pallas kernels  64.2 us (97%)
  other arithmetic  1.1 us (2%)
  local copies, waits for them, and re-layouts  0.84 us (1%)
    pallas_call x1, Pallas kernels, body(): pl.pallas_call(kernel, out_shape=jax.ShapeDtypeStruct((16, 4, 32, 128), b...  64.2 us

profile of v7, /device:TPU:1, one launch (start us, length us, event | category | flops | bytes accessed | tf_op | source)
XLA Modules:
  0.0 66.2 jit_solution(6134180138772705471)
XLA Ops:
  0.0 0.0 copy-start
  0.0 0.8 %copy-done = f32[4,32,128]{2,1,0:T(8,128)S(1)} copy-done((f32[4,32,128]{2,1,0:T(8,128)S(1)}, f32[4,32,128]{2,1,0:T(8,128)}, u32[]{:S(2)}) %copy-start) | copy-done | bytes 65560
  0.8 64.2 %shard_map.28 = bf16[16,4,32,128]{3,2,1,0:T(8,128)(2,1)S(1)} custom-call(f32[16,4,32,128]{3,2,1,0:T(8,128)} %orb_hbm.1, f32[4,32,128]{2,1,0:T(8,128)S(1)} %copy-done), custom_call_target="tpu_custom_call" | custom-call | tf_op jit(solution)/shard_map/pallas_call | solution.py:432
  65.1 1.1 %convert_element_type.3 = f32[16,4,32,128]{3,2,1,0:T(8,128)} convert(bf16[16,4,32,128]{3,2,1,0:T(8,128)(2,1)S(1)} %shard_map.28) | non-fusion elementwise | flops 262144 | bytes 1572864 | tf_op jit(solution)/shard_map/convert_element_type | solution.py:465
Async XLA Ops:
  0.0 0.8 %copy-start = (f32[4,32,128]{2,1,0:T(8,128)S(1)}, f32[4,32,128]{2,1,0:T(8,128)}, u32[]{:S(2)}) copy-start(f32[4,32,128]{2,1,0:T(8,128)} %pot_hbm.1) | copy-start | bytes 196612

commit v8 on v7

--- a/solution.py
+++ b/solution.py
@@ -60,7 +60,11 @@
             s2 = window[i] + window[i + 4]
             s1 = s1 + (src[p, o, 7:39] + src[p, o, 9:41])
             s2 = s2 + (src[p, o, 6:38] + src[p, o, 10:42])
-            w = pot[p] * window[i + 2] + (s1 + z[32 * i : 32 * i + 32] + s2 * SECOND) * FIRST
+            w = (s1 + z[32 * i : 32 * i + 32] + s2 * SECOND) * FIRST
+            if pot is None:
+                levels[k][p, o, 8:40] = w
+                continue
+            w = pot[p] * window[i + 2] + w
             w = w * 0.5 if k == 1 else w - prev[p, o, 8:40]
             if k < 6:
                 put(levels[k], p, o, w)
@@ -164,7 +168,7 @@
         for k in range(8):
             remote(potb.at[x], poth.at[yc - 5], psem.at[2], psem.at[3], (b, above + k)).start()
 
-    for i in range(1, 8):
+    for i in (4, 3, 5, 2, 6, 1, 7):
         remote(potb.at[x], potp.at[yc], psem.at[0], psem.at[1], (b, zh * 8 + (yc + i) % 8)).start()
 
     load.wait()
@@ -228,11 +232,11 @@
                 wait_bytes(send.at[0, 0], ssem.at[0, (yc + i) % 8])
 
     wait_bytes(potp.at[0:7], psem.at[1])
-    for i in range(1, 4):
+    for i in (2, 1, 3):
         along_x(i, potp, potg.at[x], 4).start()
     potg[x] = potp[...]
     wait_bytes(poth, psem.at[3])
-    for i in range(1, 4):
+    for i in (2, 1, 3):
         along_x(i, poth, poti.at[x], 6).start()
     poti[x] = poth[...]
 
@@ -255,7 +259,10 @@
     step = functools.partial(advance, levels=levels, pot=pot, circulant=circulant, sendf=sendf)
 
     def inner(o):
-        for k in range(1, 7):
+        for p in range(14, 42):
+            w = (pot[p] * levels[0][p, o, 8:40] + levels[1][p, o, 8:40]) * 0.5
+            put(levels[1], p, o, w)
+        for k in range(2, 7):
             step(k, o, [(12 + 2 * k, 32 - 4 * k)])
 
     own = b * 16 + yc * 2
@@ -289,6 +296,8 @@
 
     receive(0, (0, 7, 1, 6, 2, 5))
     receive(1, (0, 7, 1, 6))
+    for o in range(2):
+        advance(1, o, [(14, 28)], levels, None, circulant, sendf)
     wait_bytes(potg.at[0:3], psem.at[5])
 
     @pl.loop(0, 8)

time: 66.3 us -> 66.3 us (level)
  no operation moved by 1% of the time
where the time goes in v8:
time: 66.3 us; the launch traced here: 66.1 us
  Pallas kernels  64.2 us (97%)
  other arithmetic  1.1 us (2%)
  local copies, waits for them, and re-layouts  0.84 us (1%)
    pallas_call x1, Pallas kernels, body(): pl.pallas_call(kernel, out_shape=jax.ShapeDtypeStruct((16, 4, 32, 128), b...  64.2 us

profile of v8, /device:TPU:1, one launch (start us, length us, event | category | flops | bytes accessed | tf_op | source)
XLA Modules:
  0.0 66.1 jit_solution(11808516189041377979)
XLA Ops:
  0.0 0.0 copy-start
  0.0 0.8 %copy-done = f32[4,32,128]{2,1,0:T(8,128)S(1)} copy-done((f32[4,32,128]{2,1,0:T(8,128)S(1)}, f32[4,32,128]{2,1,0:T(8,128)}, u32[]{:S(2)}) %copy-start) | copy-done | bytes 65560
  0.8 64.2 %shard_map.28 = bf16[16,4,32,128]{3,2,1,0:T(8,128)(2,1)S(1)} custom-call(f32[16,4,32,128]{3,2,1,0:T(8,128)} %orb_hbm.1, f32[4,32,128]{2,1,0:T(8,128)S(1)} %copy-done), custom_call_target="tpu_custom_call" | custom-call | tf_op jit(solution)/shard_map/pallas_call | solution.py:441
  65.0 1.1 %convert_element_type.3 = f32[16,4,32,128]{3,2,1,0:T(8,128)} convert(bf16[16,4,32,128]{3,2,1,0:T(8,128)(2,1)S(1)} %shard_map.28) | non-fusion elementwise | flops 262144 | bytes 1572864 | tf_op jit(solution)/shard_map/convert_element_type | solution.py:474
Async XLA Ops:
  0.0 0.8 %copy-start = (f32[4,32,128]{2,1,0:T(8,128)S(1)}, f32[4,32,128]{2,1,0:T(8,128)}, u32[]{:S(2)}) copy-start(f32[4,32,128]{2,1,0:T(8,128)} %pot_hbm.1) | copy-start | bytes 196612
